TPU v7x, 128 devices: a whole 4x4x4 slice. The times are simulated.
128 devices in a mesh: rep: 8 (over z, core), dp: 16 (over y, x).
Axes of the slice: x: 4, y: 4, z: 4, core: 2. Of those that a mesh axis runs over, the one named last changes fastest.
Arguments:
- pixels: float32 [131072, 384], P(('rep', 'dp')), may hold values from -6 to 6
- valid_mask: int32 [131072, 384], P(('rep', 'dp')), may hold values from 0 to 1, as said below
- bottom_codes: int32 [1048576], P(('rep', 'dp')), may hold values from 0 to 511
- top_codes: int32 [262144], P(('rep', 'dp')), may hold values from 0 to 511
- params: float32 [736, 128], replicated, may hold values from -1 to 1, as said below
- first_moment: float32 [8, 736, 128], P('rep', 'dp'), may hold values from -0.00390625 to 0.00390625
- second_moment: float32 [8, 736, 128], P('rep', 'dp'), may hold values from 1e-08 to 4e-08
- outer_momentum: float32 [736, 128], P('dp'), may hold values from -0.3125 to 0.3125
- ema_counts: float32 [2, 512], replicated, may hold values from 128 to 512
- ema_sums: float32 [2, 512, 64], replicated, may hold values from -1536 to 1536
- codebooks: float32 [2, 512, 64], replicated, may hold values from -6 to 6
Outputs:
- total_loss: float32 [8], P('rep')
- valid_count: float32 [8], P('rep')
- new_params: float32 [736, 128], P('dp')
- new_first: float32 [8, 736, 128], P('rep', 'dp')
- new_second: float32 [8, 736, 128], P('rep', 'dp')
- new_momentum: float32 [736, 128], P('dp')
- new_counts: float32 [8, 2, 512], P('rep')
- new_sums: float32 [8, 2, 512, 64], P('rep')
- new_codebooks: float32 [8, 2, 512, 64], P('rep')
Inputs may be any that keep to these rules, and one draw needn't show every extreme that they name: `valid_mask`: 1 marks a valid pixel. `params`: fan-in scaled weights.
All inputs are finite; a program needn't handle non-finite values.
Results may differ from a plain program's by a relative error of at most 0.0003.
Values sent between devices are 32-bit elements; how exact they have to be, the bound alone decides.
A program may use at most 128 MiB of HBM per device.

v0:
```python
import functools
import jax
import jax.numpy as jnp
from jax import lax
from jax.experimental import pallas as pl
from jax.experimental.pallas import tpu as pltpu
from jax.sharding import PartitionSpec as P

PF = 48
EMB = 64
K = 512
STEP = 10
beta_commit = 0.25
ema_decay = 0.8
laplace_eps = 1e-05
inner_rate = 0.03
beta_first = 0.9
beta_second = 0.999
adam_eps = 1e-08
weight_decay = 0.01
outer_rate = 0.7
outer_moment = 0.9

bf16 = jnp.bfloat16
f32 = jnp.float32
O_ENC, O_RU, O_TI, O_DB, O_DT, O_RD, O_L, O_TO, O_OUT, O_END = 0, 48, 112, 368, 432, 496, 560, 624, 688, 736


def nn(a, b):
    return lax.dot_general(a, b, (((1,), (0,)), ((), ())), preferred_element_type=f32)


def nt(a, b):
    return lax.dot_general(a, b, (((1,), (1,)), ((), ())), preferred_element_type=f32)


def tn(a, b):
    return lax.dot_general(a, b, (((0,), (0,)), ((), ())), preferred_element_type=f32)


def split(v):
    hi = v.astype(bf16)
    return hi, (v - hi.astype(f32)).astype(bf16)


def pair(v):
    hi, lo = split(v)
    return jnp.concatenate([hi, lo], axis=1)


def quad(v):
    hi, lo = split(v)
    return jnp.concatenate([hi, hi, lo, lo], axis=1)


def twice(v):
    return jnp.concatenate([v, v], axis=0)


def silu_and_slope(v):
    s = 0.5 * jnp.tanh(0.5 * v) + 0.5
    a = v * s
    return a, s + a * (1.0 - s)


def lanes(parts):
    return jnp.concatenate(parts, axis=1)


def spread_codes(codes, per_row):
    a = codes.shape[0]
    rows = a * 128 // per_row
    span = 128 // per_row
    lo = (codes & 255).astype(f32).astype(bf16)
    hi = (codes >> 8).astype(f32).astype(bf16)
    up = (lax.broadcasted_iota(jnp.int32, (a, rows), 0) == lax.broadcasted_iota(jnp.int32, (a, rows), 1) // span)
    up = up.astype(f32).astype(bf16)
    keep = (
        lax.broadcasted_iota(jnp.int32, (128, rows), 0) // per_row
        == lax.broadcasted_iota(jnp.int32, (128, rows), 1) % span
    )
    pick = (
        lax.broadcasted_iota(jnp.int32, (8, 128), 0)
        == lax.broadcasted_iota(jnp.int32, (8, 128), 1) % per_row
    )
    pick = pick.astype(f32).astype(bf16)
    out = []
    for part in (lo, hi):
        wide = jnp.where(keep, tn(part, up), 0.0).astype(bf16)
        out.append(nn(pick, wide))
    return out


def swap_start(axis, n, src_at, buf, sems):
    me = lax.axis_index(axis)

    def go(k, carry):
        peer = lax.rem(me + k, n)
        pltpu.make_async_remote_copy(
            src_ref=src_at(peer), dst_ref=buf.at[me], send_sem=sems[0].at[peer], recv_sem=sems[1].at[me],
            device_id={axis: peer}, device_id_type=pl.DeviceIdType.MESH,
        ).start()
        return carry

    lax.fori_loop(1, n, go, 0)


def swap_wait(axis, n, src_at, buf, sems, recv):
    me = lax.axis_index(axis)

    def go(k, carry):
        peer = lax.rem(me + k, n)
        copy = pltpu.make_async_remote_copy(
            src_ref=src_at(peer), dst_ref=buf.at[peer], send_sem=sems[0].at[peer], recv_sem=sems[1].at[peer],
            device_id={axis: peer}, device_id_type=pl.DeviceIdType.MESH,
        )
        if recv:
            copy.wait_recv()
        else:
            copy.wait_send()
        return carry

    lax.fori_loop(1, n, go, 0)


def total(v):
    return jnp.sum(jnp.sum(v, axis=1, keepdims=True), axis=0, keepdims=True)


def in_order(buf, n):
    out = buf[0]
    for s in range(1, n):
        out = out + buf[s]
    return out


WS = {
    "enc_f": (128, 96), "ru_f": (128, 128), "ti_f": (128, 512), "db_f": (128, 256), "dt_f": (128, 256), "rd_f": (64, 256),
    "l_f": (64, 256), "to_f": (64, 256), "out_f": (48, 256), "out_b": (128, 96), "db_b": (64, 256), "dt_b": (64, 256),
    "to_b": (128, 128), "ti_b": (256, 256), "l_b": (128, 128), "ru_b": (64, 256), "rd_b": (128, 128), "book": (2, 128, 512),
}
N_DP = 16
N_REP = 8
SHARE = 46


def kernel(
    x_ref, m_ref, cb_ref, ct_ref, p_ref, first_ref, second_ref, mom_ref, cnt_ref, ema_ref, book_ref,
    loss_out, valid_out, params_out, first_out, second_out, mom_out, counts_out, sums_out, books_out,
    *scratch, R,
):
    w = dict(zip(WS, scratch))
    (
        codes_b, codes_t, acc, sacc, lacc, valid_own, valid_all, stat_own, stat_all, grad_own, grad_all, part_all,
        sums_all, step_all, par_share, *sems,
    ) = scratch[len(WS):]
    codes = (codes_b, codes_t)
    sems = [(sems[2 * i], sems[2 * i + 1]) for i in range(6)]
    sem_valid, sem_stat, sem_grad, sem_part, sem_sums, sem_step = sems
    dp = lax.axis_index("dp")
    rep = lax.axis_index("rep")

    barrier = pltpu.get_barrier_semaphore()
    for axis, n, me in (("dp", N_DP, dp), ("rep", N_REP, rep)):
        def hello(k, carry):
            pl.semaphore_signal(
                barrier, inc=1, device_id={axis: lax.rem(me + k, n)}, device_id_type=pl.DeviceIdType.MESH
            )
            return carry

        lax.fori_loop(1, n, hello, 0)

    rows = x_ref.shape[0]
    valid_own[...] = jnp.broadcast_to(total(m_ref[...].astype(f32)), (8, 128))
    valid_all[dp] = valid_own[...]
    pl.semaphore_wait(barrier, N_DP + N_REP - 2)
    valid_src = lambda peer: valid_own
    swap_start("dp", N_DP, valid_src, valid_all, sem_valid)

    par = p_ref[...]
    part = par.T
    f = lambda lo, hi: par[lo:hi]
    t = lambda lo, hi: part[:, lo:hi]
    w["enc_f"][...] = pair(t(O_ENC, O_RU))
    w["ru_f"][...] = pair(t(O_RU, O_TI))
    w["ti_f"][...] = pair(t(O_TI, O_DB))
    w["db_f"][...] = quad(t(O_DB, O_DT))
    w["dt_f"][...] = quad(t(O_DT, O_RD))
    w["rd_f"][...] = pair(f(O_RD, O_L))
    w["l_f"][...] = pair(f(O_L, O_TO))
    w["to_f"][...] = pair(f(O_TO, O_OUT))
    w["out_f"][...] = pair(f(O_OUT, O_END))
    w["out_b"][...] = pair(t(O_OUT, O_END))
    w["db_b"][...] = pair(f(O_DB, O_DT))
    w["dt_b"][...] = pair(f(O_DT, O_RD))
    w["to_b"][...] = pair(t(O_TO, O_OUT))
    w["ti_b"][...] = pair(f(O_TI, O_DB))
    w["l_b"][...] = pair(t(O_L, O_TO))
    w["ru_b"][...] = pair(f(O_RU, O_TI))
    w["rd_b"][...] = pair(t(O_RD, O_L))
    for level in (0, 1):
        hi, lo = split(book_ref[level])
        w["book"][level] = jnp.concatenate([hi, lo], axis=0)
    for ref, src, per in ((codes[0], cb_ref, 8), (codes[1], ct_ref, 2)):
        lo, hi = spread_codes(src[...], per)
        ref[0] = lo + 256.0 * hi
        ref[1] = lo + 256.0 * (1.0 - hi)
    for s in range(N_DP):
        par_share[s, 0:SHARE] = p_ref[SHARE * s : SHARE * s + SHARE]
    acc[...] = jnp.zeros_like(acc)
    sacc[...] = jnp.zeros_like(sacc)
    lacc[...] = jnp.zeros_like(lacc)
    group_rows = rows * 8 * N_DP
    swap_wait("dp", N_DP, valid_src, valid_all, sem_valid, True)
    count = in_order(valid_all, N_DP)[0:1, 0:1]
    kb = beta_commit / (group_rows * EMB) * count
    kt = beta_commit / (group_rows // 4 * EMB) * count
    ids = lax.broadcasted_iota(jnp.int32, (256, R), 0).astype(f32)

    def onehot(keys, n):
        cols = []
        for p in range(n):
            halves = [
                jnp.where(ids == keys[h][p : p + 1, :], 1.0, 0.0).astype(bf16)
                for h in (0, 1)
            ]
            cols.append(jnp.concatenate(halves, axis=0))
        return lanes(cols)

    def step(i, carry):
        at = pl.multiple_of(i * R, R)
        xt = x_ref[pl.ds(at, R), :].T
        mt = m_ref[pl.ds(at, R), :].astype(f32).T
        x = lanes([xt[48 * p : 48 * p + 48] for p in range(8)])
        m = lanes([mt[48 * p : 48 * p + 48] for p in range(8)])
        xb = x.astype(bf16)
        he, de = silu_and_slope(nn(w["enc_f"][...], twice(xb)))
        heb = he.astype(bf16)
        ar, dr = silu_and_slope(nn(w["rd_f"][...], twice(heb)))
        arb = ar.astype(bf16)
        hrb = (he + nn(w["ru_f"][...], twice(arb))).astype(bf16)
        lb = nn(w["l_f"][...], twice(hrb))
        lbb = lb.astype(bf16)
        ti = lanes([
            jnp.concatenate([lbb[:, R * p : R * p + R] for p in range(4 * g, 4 * g + 4)], axis=0) for g in (0, 1)
        ])
        ht, dt = silu_and_slope(nn(w["ti_f"][...], twice(ti)))
        htb = ht.astype(bf16)
        lt = nn(w["to_f"][...], twice(htb))
        ob = onehot([codes[0][h, :, pl.ds(at, R)] for h in (0, 1)], 8)
        ot = onehot([codes[1][h, :, pl.ds(at, R)] for h in (0, 1)], 2)
        qb2 = nn(w["book"][0], ob).astype(bf16)
        qt2 = nn(w["book"][1], ot).astype(bf16)
        ones = jnp.ones((16, 8 * R), bf16)
        sacc[0] += nt(jnp.concatenate([lbb, ones], axis=0), ob)
        sacc[1] += nt(jnp.concatenate([lt.astype(bf16), ones[:, : 2 * R]], axis=0), ot)
        gap_b = lb - (qb2[:64].astype(f32) + qb2[64:].astype(f32))
        gap_t = lt - (qt2[:64].astype(f32) + qt2[64:].astype(f32))
        top = nn(w["dt_f"][...], twice(qt2))
        pre = nn(w["db_f"][...], twice(qb2)) + lanes([top[:, R * (p // 4) : R * (p // 4) + R] for p in range(8)])
        hd, dd = silu_and_slope(pre)
        hdb = hd.astype(bf16)
        err = nn(w["out_f"][...], twice(hdb)) - x
        me = m * err
        lacc[0:48] += sum((me * err)[:, R * p : R * p + R] for p in range(8))
        lacc[48:112] += sum((gap_b * gap_b)[:, R * p : R * p + R] for p in range(8))
        lacc[112:176] += sum((gap_t * gap_t)[:, R * p : R * p + R] for p in range(2))
        grb = me.astype(bf16)
        acc[O_OUT:O_END] += nt(grb, hdb)
        gpd = nn(w["out_b"][...], twice(grb)) * dd
        gpdb = gpd.astype(bf16)
        g = nt(qb2, gpdb)
        acc[O_DB:O_DT] += g[:64] + g[64:]
        gtrb = lanes([sum(gpd[:, R * p : R * p + R] for p in range(4 * g_, 4 * g_ + 4)) for g_ in (0, 1)]).astype(bf16)
        g = nt(qt2, gtrb)
        acc[O_DT:O_RD] += g[:64] + g[64:]
        gltb = (nn(w["dt_b"][...], twice(gtrb)) + kt * gap_t).astype(bf16)
        acc[O_TO:O_OUT] += nt(gltb, htb)
        gptb = (nn(w["to_b"][...], twice(gltb)) * dt).astype(bf16)
        acc[O_TI:O_DB] += nt(ti, gptb)
        gti = nn(w["ti_b"][...], twice(gptb))
        gti = lanes([gti[64 * (p % 4) : 64 * (p % 4) + 64, R * (p // 4) : R * (p // 4) + R] for p in range(8)])
        glbb = (nn(w["db_b"][...], twice(gpdb)) + gti + kb * gap_b).astype(bf16)
        acc[O_L:O_TO] += nt(glbb, hrb)
        ghr = nn(w["l_b"][...], twice(glbb))
        ghrb = ghr.astype(bf16)
        acc[O_RU:O_TI] += nt(arb, ghrb)
        gprb = (nn(w["ru_b"][...], twice(ghrb)) * dr).astype(bf16)
        acc[O_RD:O_L] += nt(gprb, heb)
        gpeb = ((ghr + nn(w["rd_b"][...], twice(gprb))) * de).astype(bf16)
        acc[O_ENC:O_RU] += nt(xb, gpeb)
        return carry

    lax.fori_loop(0, rows // R, step, 0)

    scale = 2.0 / count
    for s in range(N_DP):
        grad_own[s, 0:SHARE] = acc[SHARE * s : SHARE * s + SHARE] * scale
    grad_src = lambda peer: grad_own.at[peer]
    swap_start("dp", N_DP, grad_src, grad_all, sem_grad)
    part_src = lambda peer: sacc.at[peer // 8, pl.ds(pl.multiple_of(8 * lax.rem(peer, 8), 8), 8)]
    swap_start("dp", N_DP, part_src, part_all, sem_part)
    one = lambda v: jnp.broadcast_to(total(v), (1, 128))
    stat_own[...] = jnp.concatenate(
        [sacc[level][64:65, 128 * j : 128 * j + 128] for level in (0, 1) for j in range(4)]
        + [one(lacc[0:48]), one(lacc[48:112]), one(lacc[112:176]), jnp.zeros((5, 128), f32)], axis=0
    )
    stat_src = lambda peer: stat_own
    swap_start("dp", N_DP, stat_src, stat_all, sem_stat)
    grad_all[dp] = grad_own[dp]
    part_all[dp] = part_src(dp)[...]
    stat_all[dp] = stat_own[...]

    swap_wait("dp", N_DP, grad_src, grad_all, sem_grad, True)
    grads = in_order(grad_all, N_DP)[0:SHARE]
    own = par_share[dp][0:SHARE]
    first_new = beta_first * first_ref[0] + (1.0 - beta_first) * grads
    second_new = beta_second * second_ref[0] + (1.0 - beta_second) * grads * grads
    first_out[0] = first_new
    second_out[0] = second_new
    bias_first = 1.0 - beta_first**STEP
    bias_second = 1.0 - beta_second**STEP
    step_here = inner_rate * (
        first_new / bias_first / (jnp.sqrt(second_new / bias_second) + adam_eps) + weight_decay * own
    )
    step_all[rep, 0:SHARE] = step_here
    step_src = lambda peer: step_all.at[rep]
    swap_start("rep", N_REP, step_src, step_all, sem_step)

    swap_wait("dp", N_DP, part_src, part_all, sem_part, True)
    sums_all[dp] = in_order(part_all, N_DP)
    sums_src = lambda peer: sums_all.at[dp]
    swap_start("dp", N_DP, sums_src, sums_all, sem_sums)
    swap_wait("dp", N_DP, stat_src, stat_all, sem_stat, True)
    stats = in_order(stat_all, N_DP)
    seen = jnp.concatenate([lanes([stats[4 * level + j : 4 * level + j + 1] for j in range(4)]) for level in (0, 1)], axis=0)
    counts_new = ema_decay * cnt_ref[...] + (1.0 - ema_decay) * seen
    counts_out[0] = counts_new
    totals = jnp.sum(counts_new, axis=1, keepdims=True)
    smooth = (counts_new + laplace_eps) / (totals + K * laplace_eps) * totals
    loss = stats[8:9, 0:1] / count + beta_commit * (
        stats[9:10, 0:1] / (group_rows * EMB) + stats[10:11, 0:1] / (group_rows // 4 * EMB)
    )
    loss_out[0] = jnp.sum(loss)
    valid_out[0] = jnp.sum(count)

    swap_wait("rep", N_REP, step_src, step_all, sem_step, True)
    mean_delta = in_order(step_all, N_REP)[0:SHARE] * (1.0 / N_REP)
    momentum_new = outer_moment * mom_ref[...] + mean_delta
    mom_out[...] = momentum_new
    params_out[...] = own - outer_rate * (mean_delta + outer_moment * momentum_new)

    swap_wait("dp", N_DP, sums_src, sums_all, sem_sums, True)
    for level in (0, 1):
        inverse = 1.0 / smooth[level : level + 1]
        for j in range(8):
            rows_j = slice(8 * j, 8 * j + 8)
            sums_new = ema_decay * ema_ref[level, rows_j] + (1.0 - ema_decay) * sums_all[8 * level + j]
            sums_out[0, level, rows_j] = sums_new
            books_out[0, level, rows_j] = sums_new * inverse

    for axis, n, src, buf, sem in (
        ("dp", N_DP, valid_src, valid_all, sem_valid), ("dp", N_DP, grad_src, grad_all, sem_grad),
        ("dp", N_DP, part_src, part_all, sem_part), ("dp", N_DP, stat_src, stat_all, sem_stat),
        ("rep", N_REP, step_src, step_all, sem_step), ("dp", N_DP, sums_src, sums_all, sem_sums),
    ):
        swap_wait(axis, n, src, buf, sem, False)


def shards(
    pixels, valid_mask, bottom_codes, top_codes, params, first_moment, second_moment, outer_momentum, ema_counts,
    ema_sums, codebooks, *, R,
):
    rows = pixels.shape[0]
    vm = pl.BlockSpec(memory_space=pltpu.VMEM)
    sm = pl.BlockSpec(memory_space=pltpu.SMEM)
    shape = lambda *s: jax.ShapeDtypeStruct(s, f32)
    dma = pltpu.SemaphoreType.DMA
    outs = pl.pallas_call(
        functools.partial(kernel, R=R),
        out_shape=(
            shape(1), shape(1), shape(SHARE, 128), shape(1, SHARE, 128), shape(1, SHARE, 128), shape(SHARE, 128),
            shape(1, 2, K), shape(1, 2, EMB, K), shape(1, 2, EMB, K),
        ),
        in_specs=[vm] * 11,
        out_specs=(sm, sm) + (vm,) * 7,
        scratch_shapes=[pltpu.VMEM(s, bf16) for s in WS.values()]
        + [pltpu.VMEM((2, 8, rows), f32)] * 2
        + [
            pltpu.VMEM((736, 128), f32), pltpu.VMEM((2, 80, 512), f32), pltpu.VMEM((176, R), f32),
            pltpu.VMEM((8, 128), f32), pltpu.VMEM((N_DP, 8, 128), f32),
            pltpu.VMEM((16, 128), f32), pltpu.VMEM((N_DP, 16, 128), f32),
            pltpu.VMEM((N_DP, 48, 128), f32), pltpu.VMEM((N_DP, 48, 128), f32),
            pltpu.VMEM((N_DP, 8, 512), f32), pltpu.VMEM((N_DP, 8, 512), f32),
            pltpu.VMEM((N_REP, 48, 128), f32), pltpu.VMEM((N_DP, 48, 128), f32),
        ]
        + [dma((N_DP,))] * 10 + [dma((N_REP,))] * 2,
        compiler_params=pltpu.CompilerParams(
            vmem_limit_bytes=56 * 2**20, collective_id=0, has_side_effects=True
        ),
    )(
        pixels, valid_mask, bottom_codes.reshape(-1, 128), top_codes.reshape(-1, 128), params, first_moment,
        second_moment, outer_momentum, ema_counts, jnp.swapaxes(ema_sums, 1, 2), jnp.swapaxes(codebooks, 1, 2),
    )
    return outs[:7] + (jnp.swapaxes(outs[7], 2, 3), jnp.swapaxes(outs[8], 2, 3))


def solution(mesh):
    return jax.shard_map(
        functools.partial(shards, R=256),
        mesh=mesh,
        in_specs=(
            P(("rep", "dp"), None),
            P(("rep", "dp"), None),
            P(("rep", "dp")),
            P(("rep", "dp")),
            P(),
            P("rep", "dp", None),
            P("rep", "dp", None),
            P("dp", None),
            P(),
            P(),
            P(),
        ),
        out_specs=(
            P("rep"),
            P("rep"),
            P("dp", None),
            P("rep", "dp", None),
            P("rep", "dp", None),
            P("dp", None),
            P("rep", None, None),
            P("rep", None, None, None),
            P("rep", None, None, None),
        ),
        check_vma=False,
    )
```

profile of v0, /device:TPU:0, one launch (start us, length us, event | category | flops | bytes accessed | tf_op | source)
XLA Modules:
  0.0 69.8 jit_solution(1351064359533119997)
XLA Ops:
  0.6 1.3 %copy.20.first_ref = f32[1,46,128]{2,1,0:T(8,128)} copy(f32[1,46,128]{2,0,1:T(1,128)} %param.16) | data formatting | bytes 47104 | tf_op args[5]
  2.0 1.3 %copy.21.second_ref = f32[1,46,128]{2,1,0:T(8,128)} copy(f32[1,46,128]{2,0,1:T(1,128)} %param.17) | data formatting | bytes 47104 | tf_op args[6]
  3.3 52.9 %shard_map.178 = (f32[1]{0:T(128)}, f32[1]{0:T(128)}, f32[46,128]{1,0:T(8,128)}, f32[1,46,128]{2,1,0:T(8,128)}, f32[1,46,128]{2,1,0:T(8,128)}, /*index=5*/f32[46...) custom-call(f32[1024,384]{1,0:T(8,128)} %x_ref.1, s32[1024,384]{1,0:T(8,128)} %m_ref.1, ...), custom_call_target="tpu_custom_call" | custom-call | tf_op jit(solution)/shard_map/pallas_call | solution.py:379
  56.2 1.4 %copy.22 = f32[1,46,128]{2,0,1:T(1,128)} copy(f32[1,46,128]{2,1,0:T(8,128)} %get-tuple-element.30) | data formatting | bytes 47104
  57.6 1.4 %copy.23 = f32[1,46,128]{2,0,1:T(1,128)} copy(f32[1,46,128]{2,1,0:T(8,128)} %get-tuple-element.31) | data formatting | bytes 47104
  60.2 1.3 %copy.33 = f32[46,128]{1,0:T(8,128)} copy(f32[46,128]{1,0:T(8,128)} %get-tuple-element.47) | data formatting | bytes 47104
  61.5 1.3 %copy.34 = f32[46,128]{1,0:T(8,128)} copy(f32[46,128]{1,0:T(8,128)} %get-tuple-element.50) | data formatting | bytes 47104
  62.9 1.3 %copy.35 = f32[1,2,512]{2,1,0:T(2,128)} copy(f32[1,2,512]{2,1,0:T(2,128)} %get-tuple-element.51) | data formatting | bytes 8192
  64.2 1.7 %copy.36 = f32[1,2,512,64]{2,3,1,0:T(8,128)} copy(f32[1,2,512,64]{2,3,1,0:T(8,128)} %bitcast.9) | data formatting | bytes 524288
  65.8 1.7 %copy.37 = f32[1,2,512,64]{2,3,1,0:T(8,128)} copy(f32[1,2,512,64]{2,3,1,0:T(8,128)} %bitcast.8) | data formatting | bytes 524288
where the time goes:
time: 70.4 us; the launch traced here: 69.8 us
  Pallas kernels  52.9 us (75%)
  local copies, waits for them, and re-layouts  12.7 us (18%)
  between operations  4.13 us (6%)
    pallas_call x1, Pallas kernels, shards(): pl.pallas_call(functools.partial(kernel, R=R), out_shape=(shape(1), shape...  52.9 us
    unnamed x9, local copies, waits for them, and re-layouts  12.7 us

commit v1 on v0

v1 whole, which is shorter than its diff:
```python
import functools
import jax
import jax.numpy as jnp
from jax import lax
from jax.experimental import pallas as pl
from jax.experimental.pallas import tpu as pltpu
from jax.sharding import PartitionSpec as P

PF = 48
EMB = 64
K = 512
STEP = 10
beta_commit = 0.25
ema_decay = 0.8
laplace_eps = 1e-05
inner_rate = 0.03
beta_first = 0.9
beta_second = 0.999
adam_eps = 1e-08
weight_decay = 0.01
outer_rate = 0.7
outer_moment = 0.9

bf16 = jnp.bfloat16
f32 = jnp.float32
O_ENC, O_RU, O_TI, O_DB, O_DT, O_RD, O_L, O_TO, O_OUT, O_END = 0, 48, 112, 368, 432, 496, 560, 624, 688, 736


def nn(a, b):
    return lax.dot_general(a, b, (((1,), (0,)), ((), ())), preferred_element_type=f32)


def nt(a, b):
    return lax.dot_general(a, b, (((1,), (1,)), ((), ())), preferred_element_type=f32)


def tn(a, b):
    return lax.dot_general(a, b, (((0,), (0,)), ((), ())), preferred_element_type=f32)


def split(v):
    hi = v.astype(bf16)
    return hi, (v - hi.astype(f32)).astype(bf16)


def pair(v):
    hi, lo = split(v)
    return jnp.concatenate([hi, lo], axis=1)


def quad(v):
    hi, lo = split(v)
    return jnp.concatenate([hi, hi, lo, lo], axis=1)


def twice(v):
    return jnp.concatenate([v, v], axis=0)


def silu_and_slope(v):
    s = 0.5 * jnp.tanh(0.5 * v) + 0.5
    a = v * s
    return a, s + a * (1.0 - s)


def lanes(parts):
    return jnp.concatenate(parts, axis=1)


def spread_codes(codes, per_row):
    a = codes.shape[0]
    rows = a * 128 // per_row
    span = 128 // per_row
    lo = (codes & 255).astype(f32).astype(bf16)
    hi = (codes >> 8).astype(f32).astype(bf16)
    up = (lax.broadcasted_iota(jnp.int32, (a, rows), 0) == lax.broadcasted_iota(jnp.int32, (a, rows), 1) // span)
    up = up.astype(f32).astype(bf16)
    keep = (
        lax.broadcasted_iota(jnp.int32, (128, rows), 0) // per_row
        == lax.broadcasted_iota(jnp.int32, (128, rows), 1) % span
    )
    pick = (
        lax.broadcasted_iota(jnp.int32, (8, 128), 0)
        == lax.broadcasted_iota(jnp.int32, (8, 128), 1) % per_row
    )
    pick = pick.astype(f32).astype(bf16)
    out = []
    for part in (lo, hi):
        wide = jnp.where(keep, tn(part, up), 0.0).astype(bf16)
        out.append(nn(pick, wide))
    return out


def stack(v):
    hi, lo = split(v)
    return jnp.concatenate([hi, lo], axis=0)


def halves(v):
    n = v.shape[0] // 2
    return v[:n] + v[n:]


def exact(a, b, dims):
    return lax.dot_general(a, b, ((dims), ((), ())), precision=lax.Precision.HIGHEST, preferred_element_type=f32)


WS = {
    "enc_f": (128, 96), "rd_f": (128, 128), "l_f": (128, 192), "ti_f": (128, 512), "to_f": (128, 128), "db_f": (128, 256),
    "dt_f": (128, 256), "out_f": (96, 128), "out_b": (128, 96), "db_b": (128, 128), "dt_b": (128, 128), "to_b": (128, 128),
    "ti_b": (256, 256), "ru_b": (64, 128), "he_b": (128, 256), "book_b": (128, 512), "book_t": (128, 512),
}
KEEP = {
    "x": (48, 8, bf16), "he": (128, 8, bf16), "de": (128, 8, bf16), "ar": (64, 8, bf16), "dr": (64, 8, bf16),
    "gap_b": (64, 8, bf16), "gl": (64, 8, f32),
}
KEEP_TOP = {
    "ti": (256, bf16), "ht": (128, bf16), "dt": (128, bf16), "gap_t": (64, f32), "gt": (64, f32),
}
ACC = {
    "e": (128, 48), "he": (128, 128), "ar": (64, 64), "ti": (256, 128), "to": (128, 64), "db": (128, 128), "dt": (128, 128),
    "out": (128, 48), "sum_b": (80, 512), "sum_t": (80, 512),
}


def weights(par, book_ref, w):
    part = par.T
    f = lambda lo, hi: par[lo:hi]
    t = lambda lo, hi: part[:, lo:hi]
    w["enc_f"][...] = pair(t(O_ENC, O_RU))
    w["rd_f"][...] = stack(f(O_RD, O_L))
    cross = exact(f(O_L, O_TO), f(O_RU, O_TI), ((1,), (1,)))
    w["l_f"][...] = stack(lanes([f(O_L, O_TO), cross]))
    w["ti_f"][...] = pair(t(O_TI, O_DB))
    w["to_f"][...] = stack(f(O_TO, O_OUT))
    w["db_f"][...] = quad(t(O_DB, O_DT))
    w["dt_f"][...] = quad(t(O_DT, O_RD))
    w["out_f"][...] = stack(f(O_OUT, O_END))
    w["out_b"][...] = pair(t(O_OUT, O_END))
    w["db_b"][...] = stack(f(O_DB, O_DT))
    w["dt_b"][...] = stack(f(O_DT, O_RD))
    w["to_b"][...] = pair(t(O_TO, O_OUT))
    w["ti_b"][...] = pair(f(O_TI, O_DB))
    w["ru_b"][...] = pair(exact(f(O_RU, O_TI), f(O_L, O_TO), ((1,), (1,))))
    w["he_b"][...] = pair(lanes([t(O_L, O_TO), t(O_RD, O_L)]))
    w["book_b"][...] = stack(book_ref[0])
    w["book_t"][...] = stack(book_ref[1])


def code_keys(rows_ref, cols_ref, src, per):
    lo, hi = spread_codes(src[...], per)
    for h, key in ((0, lo + 256.0 * hi), (1, lo + 256.0 * (1.0 - hi))):
        rows_ref[h] = key
        cols_ref[h] = key.T


def hot(equal):
    return jnp.where(equal, jnp.ones((), bf16), jnp.zeros((), bf16))


def forward(i, R, x_ref, m_ref, codes, w, keep, acc, lacc):
    down = lax.broadcasted_iota(jnp.int32, (256, R), 0).astype(f32).astype(bf16)
    along = lax.broadcasted_iota(jnp.int32, (R, 256), 1).astype(f32).astype(bf16)
    at = pl.multiple_of(i * R, R)
    tops = pl.ds(pl.multiple_of(i * 2 * R, 2 * R), 2 * R)

    def by_code(level, n):
        key = [codes[level][0][h, :, pl.ds(at, R)] for h in (0, 1)]
        return lanes([
            jnp.concatenate([hot(down == key[h][p : p + 1, :].astype(bf16)) for h in (0, 1)], axis=0) for p in range(n)
        ])

    def by_patch(level, n):
        key = [codes[level][1][h, pl.ds(at, R), :] for h in (0, 1)]
        return jnp.concatenate([
            lanes([hot(along == jnp.broadcast_to(key[h][:, p : p + 1], (R, 256)).astype(bf16)) for h in (0, 1)]) for p in range(n)
        ], axis=0)

    xt = x_ref[pl.ds(at, R), :].T
    mt = m_ref[pl.ds(at, R), :].astype(f32).T
    x = lanes([xt[48 * p : 48 * p + 48] for p in range(8)])
    m = lanes([mt[48 * p : 48 * p + 48] for p in range(8)])
    xb = x.astype(bf16)
    keep["x"][i] = xb
    he, de = silu_and_slope(nn(w["enc_f"][...], twice(xb)))
    heb = he.astype(bf16)
    keep["he"][i] = heb
    keep["de"][i] = de.astype(bf16)
    ar, dr = silu_and_slope(halves(nn(w["rd_f"][...], heb)))
    arb = ar.astype(bf16)
    keep["ar"][i] = arb
    keep["dr"][i] = dr.astype(bf16)
    lb = halves(nn(w["l_f"][...], jnp.concatenate([heb, arb], axis=0)))
    lbb = lb.astype(bf16)
    ti = lanes([
        jnp.concatenate([lbb[:, R * p : R * p + R] for p in range(4 * g, 4 * g + 4)], axis=0) for g in (0, 1)
    ])
    keep["ti"][:, tops] = ti
    ht, dt = silu_and_slope(nn(w["ti_f"][...], twice(ti)))
    htb = ht.astype(bf16)
    keep["ht"][:, tops] = htb
    keep["dt"][:, tops] = dt.astype(bf16)
    lt = halves(nn(w["to_f"][...], htb))
    qb2 = nn(w["book_b"][...], by_code(0, 8)).astype(bf16)
    qt2 = nn(w["book_t"][...], by_code(1, 2)).astype(bf16)
    ones = jnp.ones((16, 8 * R), bf16)
    acc["sum_b"][...] += nn(jnp.concatenate([lbb, ones], axis=0), by_patch(0, 8))
    acc["sum_t"][...] += nn(jnp.concatenate([lt.astype(bf16), ones[:, : 2 * R]], axis=0), by_patch(1, 2))
    gap_b = lb - halves(qb2.astype(f32))
    gap_t = lt - halves(qt2.astype(f32))
    keep["gap_b"][i] = gap_b.astype(bf16)
    keep["gap_t"][:, tops] = gap_t
    top = nn(w["dt_f"][...], twice(qt2))
    pre = nn(w["db_f"][...], twice(qb2)) + lanes([top[:, R * (p // 4) : R * (p // 4) + R] for p in range(8)])
    hd, dd = silu_and_slope(pre)
    hdb = hd.astype(bf16)
    err = halves(nn(w["out_f"][...], hdb)) - x
    me = m * err
    lacc[0:48] += sum((me * err)[:, R * p : R * p + R] for p in range(8))
    lacc[48:112] += sum((gap_b * gap_b)[:, R * p : R * p + R] for p in range(8))
    lacc[112:176] += sum((gap_t * gap_t)[:, R * p : R * p + R] for p in range(2))
    grb = me.astype(bf16)
    acc["out"][...] += nt(hdb, grb)
    gpd = nn(w["out_b"][...], twice(grb)) * dd
    gpdb = gpd.astype(bf16)
    acc["db"][...] += nt(qb2, gpdb)
    gtrb = lanes([sum(gpd[:, R * p : R * p + R] for p in range(4 * g_, 4 * g_ + 4)) for g_ in (0, 1)]).astype(bf16)
    acc["dt"][...] += nt(qt2, gtrb)
    keep["gt"][:, tops] = halves(nn(w["dt_b"][...], gtrb))
    keep["gl"][i] = halves(nn(w["db_b"][...], gpdb))


def top_backward(n, R, kt, w, keep, acc):
    gltb = (keep["gt"][...] + kt * keep["gap_t"][...]).astype(bf16)
    acc["to"][...] = nt(keep["ht"][...], gltb)
    gptb = (nn(w["to_b"][...], twice(gltb)) * keep["dt"][...].astype(f32)).astype(bf16)
    acc["ti"][...] = nt(keep["ti"][...], gptb)
    gti = nn(w["ti_b"][...], twice(gptb))
    for i in range(n):
        for p in range(8):
            at = 2 * R * i + R * (p // 4)
            keep["gl"][i, :, R * p : R * p + R] += gti[64 * (p % 4) : 64 * (p % 4) + 64, at : at + R]


def backward(i, kb, w, keep, acc):
    glbb = (keep["gl"][i] + kb * keep["gap_b"][i].astype(f32)).astype(bf16)
    gprb = (nn(w["ru_b"][...], twice(glbb)) * keep["dr"][i].astype(f32)).astype(bf16)
    both = jnp.concatenate([glbb, gprb], axis=0)
    acc["he"][...] += nt(both, keep["he"][i])
    acc["ar"][...] += nt(glbb, keep["ar"][i])
    gpeb = (nn(w["he_b"][...], twice(both)) * keep["de"][i].astype(f32)).astype(bf16)
    acc["e"][...] += nt(gpeb, keep["x"][i])


def gradients(par, acc, scale):
    cross = acc["ar"][...]
    w_ru, w_l = par[O_RU:O_TI], par[O_L:O_TO]
    pieces = [
        acc["e"][...].T,
        exact(cross, w_l, ((0,), (0,))),
        acc["ti"][...],
        halves(acc["db"][...]),
        halves(acc["dt"][...]),
        acc["he"][64:128],
        acc["he"][0:64] + exact(cross, w_ru, ((1,), (0,))),
        acc["to"][...].T,
        acc["out"][...].T,
    ]
    return jnp.concatenate(pieces, axis=0) * scale


def scratches(rows, R):
    return (
        [pltpu.VMEM(s, bf16) for s in WS.values()]
        + [pltpu.VMEM((rows // R, c, n * R), t) for c, n, t in KEEP.values()]
        + [pltpu.VMEM((c, rows * 2), t) for c, t in KEEP_TOP.values()]
        + [pltpu.VMEM(s, f32) for s in ACC.values()]
        + [pltpu.VMEM((2, 8, rows), f32), pltpu.VMEM((2, rows, 8), f32)] * 2
        + [pltpu.VMEM((176, R), f32)]
    )


def unscratch(scratch):
    scratch = list(scratch)
    take = lambda names: {k: scratch.pop(0) for k in names}
    w, keep, acc = take(WS), take(list(KEEP) + list(KEEP_TOP)), take(ACC)
    codes = ((scratch.pop(0), scratch.pop(0)), (scratch.pop(0), scratch.pop(0)))
    return w, keep, acc, codes, scratch


def swap_start(axis, n, src_at, buf, sems):
    me = lax.axis_index(axis)

    def go(k, carry):
        peer = lax.rem(me + k, n)
        pltpu.make_async_remote_copy(
            src_ref=src_at(peer), dst_ref=buf.at[me], send_sem=sems[0].at[peer], recv_sem=sems[1].at[me],
            device_id={axis: peer}, device_id_type=pl.DeviceIdType.MESH,
        ).start()
        return carry

    lax.fori_loop(1, n, go, 0)


def swap_wait(axis, n, src_at, buf, sems, recv):
    me = lax.axis_index(axis)

    def go(k, carry):
        peer = lax.rem(me + k, n)
        copy = pltpu.make_async_remote_copy(
            src_ref=src_at(peer), dst_ref=buf.at[peer], send_sem=sems[0].at[peer], recv_sem=sems[1].at[peer],
            device_id={axis: peer}, device_id_type=pl.DeviceIdType.MESH,
        )
        if recv:
            copy.wait_recv()
        else:
            copy.wait_send()
        return carry

    lax.fori_loop(1, n, go, 0)


def total(v):
    return jnp.sum(jnp.sum(v, axis=1, keepdims=True), axis=0, keepdims=True)


def in_order(buf, n):
    out = buf[0]
    for s in range(1, n):
        out = out + buf[s]
    return out

N_DP = 16
N_REP = 8
SHARE = 46
EARLY = (3, 4, 5, 6, 7, 8, 9, 14, 15)
LATE = (0, 1, 2, 10, 11, 12, 13)


def share_start(shares, src, buf, sems):
    me = lax.axis_index("dp")
    for s in shares:
        @pl.when(me != s)
        def _():
            pltpu.make_async_remote_copy(
                src_ref=src.at[s], dst_ref=buf.at[me], send_sem=sems[0].at[s], recv_sem=sems[1].at[me],
                device_id={"dp": s}, device_id_type=pl.DeviceIdType.MESH,
            ).start()


def grad_pieces(par, acc, scale, late):
    if late:
        cross = acc["ar"][...]
        w_ru, w_l = par[O_RU:O_TI], par[O_L:O_TO]
        pieces = [
            (O_ENC, acc["e"][...].T),
            (O_RU, exact(cross, w_l, ((0,), (0,)))),
            (O_RD, acc["he"][64:128]),
            (O_L, acc["he"][0:64] + exact(cross, w_ru, ((1,), (0,)))),
        ]
    else:
        pieces = [
            (O_TI, acc["ti"][...]),
            (O_DB, halves(acc["db"][...])),
            (O_DT, halves(acc["dt"][...])),
            (O_TO, acc["to"][...].T),
            (O_OUT, acc["out"][...].T),
        ]
    return [(at, v * scale) for at, v in pieces]


def put_rows(ref, at, v):
    end = at + v.shape[0]
    for s in range(N_DP):
        lo, hi = max(at, SHARE * s), min(end, SHARE * s + SHARE)
        if lo < hi:
            ref[s, lo - SHARE * s : hi - SHARE * s] = v[lo - at : hi - at]


def kernel(
    x_hbm, m_hbm, cb_ref, ct_ref, p_ref, first_ref, second_ref, mom_ref, cnt_ref, ema_ref, book_ref,
    scal_out, params_out, first_out, second_out, mom_out, counts_out, sums_out, books_out,
    *scratch, R,
):
    w, keep, acc, codes, scratch = unscratch(scratch)
    (
        lacc, x_ref, m_ref, valid_own, valid_all, stat_own, stat_all, grad_own, grad_all, part_own, part_all, sums_all, step_all,
        par_share, in_sems, *sems,
    ) = scratch
    sems = [(sems[2 * i], sems[2 * i + 1]) for i in range(6)]
    sem_valid, sem_stat, sem_grad, sem_part, sem_sums, sem_step = sems
    dp = lax.axis_index("dp")
    rep = lax.axis_index("rep")
    rows = x_ref.shape[0]
    n = rows // R

    m_copy = pltpu.make_async_copy(m_hbm, m_ref, in_sems.at[0])
    x_copy = pltpu.make_async_copy(x_hbm, x_ref, in_sems.at[1])
    m_copy.start()
    x_copy.start()

    barrier = pltpu.get_barrier_semaphore()
    for axis, size, me in (("dp", N_DP, dp), ("rep", N_REP, rep)):
        def hello(k, carry):
            pl.semaphore_signal(
                barrier, inc=1, device_id={axis: lax.rem(me + k, size)}, device_id_type=pl.DeviceIdType.MESH
            )
            return carry

        lax.fori_loop(1, size, hello, 0)

    weights(p_ref[...], book_ref, w)
    code_keys(*codes[0], cb_ref, 8)
    code_keys(*codes[1], ct_ref, 2)
    for v in acc.values():
        v[...] = jnp.zeros_like(v)
    lacc[...] = jnp.zeros_like(lacc)
    for s in range(N_DP):
        par_share[s, 0:SHARE] = p_ref[SHARE * s : SHARE * s + SHARE]
        grad_own[s] = jnp.zeros((48, 128), f32)
    m_copy.wait()
    valid_own[...] = jnp.broadcast_to(total(m_ref[...].astype(f32)), (8, 128))
    valid_all[dp] = valid_own[...]
    valid_src = lambda peer: valid_own
    x_copy.wait()

    def go_forward(i, carry):
        @pl.when(i == 1)
        def _():
            pl.semaphore_wait(barrier, N_DP + N_REP - 2)
            swap_start("dp", N_DP, valid_src, valid_all, sem_valid)

        forward(i, R, x_ref, m_ref, codes, w, keep, acc, lacc)
        return carry

    lax.fori_loop(0, n, go_forward, 0)

    for d in range(N_DP):
        part_own[d] = acc["sum_b" if d < 8 else "sum_t"][8 * (d % 8) : 8 * (d % 8) + 8]
    part_src = lambda peer: part_own.at[peer]
    swap_start("dp", N_DP, part_src, part_all, sem_part)
    one = lambda v: jnp.broadcast_to(total(v), (1, 128))
    stat_own[...] = jnp.concatenate(
        [acc[name][64:65, 128 * j : 128 * j + 128] for name in ("sum_b", "sum_t") for j in range(4)]
        + [one(lacc[0:48]), one(lacc[48:112]), one(lacc[112:176]), jnp.zeros((5, 128), f32)], axis=0
    )
    stat_src = lambda peer: stat_own
    swap_start("dp", N_DP, stat_src, stat_all, sem_stat)
    part_all[dp] = part_own[dp]
    stat_all[dp] = stat_own[...]

    group_rows = rows * 8 * N_DP
    swap_wait("dp", N_DP, valid_src, valid_all, sem_valid, True)
    count = in_order(valid_all, N_DP)[0:1, 0:1]
    scale = 2.0 / count
    kb = beta_commit / (group_rows * EMB) * count
    kt = beta_commit / (group_rows // 4 * EMB) * count
    top_backward(n, R, kt, w, keep, acc)
    for at, v in grad_pieces(p_ref, acc, scale, False):
        put_rows(grad_own, at, v)
    share_start(EARLY, grad_own, grad_all, sem_grad)

    def go_backward(i, carry):
        backward(i, kb, w, keep, acc)
        return carry

    lax.fori_loop(0, n, go_backward, 0)
    for at, v in grad_pieces(p_ref, acc, scale, True):
        put_rows(grad_own, at, v)
    share_start(LATE, grad_own, grad_all, sem_grad)
    grad_src = lambda peer: grad_own.at[peer]
    grad_all[dp] = grad_own[dp]

    swap_wait("dp", N_DP, part_src, part_all, sem_part, True)
    sums_all[dp] = in_order(part_all, N_DP)
    sums_src = lambda peer: sums_all.at[dp]
    swap_start("dp", N_DP, sums_src, sums_all, sem_sums)

    swap_wait("dp", N_DP, grad_src, grad_all, sem_grad, True)
    grads = in_order(grad_all, N_DP)[0:SHARE]
    own = par_share[dp][0:SHARE]
    first_new = beta_first * first_ref[:, 0, :] + (1.0 - beta_first) * grads
    second_new = beta_second * second_ref[:, 0, :] + (1.0 - beta_second) * grads * grads
    bias_first = 1.0 - beta_first**STEP
    bias_second = 1.0 - beta_second**STEP
    step_here = inner_rate * (
        first_new / bias_first / (jnp.sqrt(second_new / bias_second) + adam_eps) + weight_decay * own
    )
    step_all[rep, 0:SHARE] = step_here
    step_all[rep, SHARE:48] = jnp.zeros((48 - SHARE, 128), f32)
    step_src = lambda peer: step_all.at[rep]
    swap_start("rep", N_REP, step_src, step_all, sem_step)
    first_out[:, 0, :] = first_new
    second_out[:, 0, :] = second_new

    swap_wait("dp", N_DP, stat_src, stat_all, sem_stat, True)
    stats = in_order(stat_all, N_DP)
    seen = jnp.concatenate([lanes([stats[4 * level + j : 4 * level + j + 1] for j in range(4)]) for level in (0, 1)], axis=0)
    counts_new = ema_decay * cnt_ref[...] + (1.0 - ema_decay) * seen
    counts_out[0] = counts_new
    totals = jnp.sum(counts_new, axis=1, keepdims=True)
    smooth = (counts_new + laplace_eps) / (totals + K * laplace_eps) * totals
    loss = stats[8:9, 0:1] / count + beta_commit * (
        stats[9:10, 0:1] / (group_rows * EMB) + stats[10:11, 0:1] / (group_rows // 4 * EMB)
    )
    scal_out[...] = jnp.concatenate([jnp.broadcast_to(loss, (1, 128)), jnp.broadcast_to(count, (1, 128)), jnp.zeros((6, 128), f32)], axis=0)

    swap_wait("dp", N_DP, sums_src, sums_all, sem_sums, True)
    for level in (0, 1):
        inverse = 1.0 / smooth[level : level + 1]
        for j in range(8):
            rows_j = slice(8 * j, 8 * j + 8)
            sums_new = ema_decay * ema_ref[level, rows_j] + (1.0 - ema_decay) * sums_all[8 * level + j]
            sums_out[0, level, rows_j] = sums_new
            books_out[0, level, rows_j] = sums_new * inverse

    swap_wait("rep", N_REP, step_src, step_all, sem_step, True)
    mean_delta = in_order(step_all, N_REP)[0:SHARE] * (1.0 / N_REP)
    momentum_new = outer_moment * mom_ref[...] + mean_delta
    mom_out[...] = momentum_new
    params_out[...] = own - outer_rate * (mean_delta + outer_moment * momentum_new)

    for axis, size, src, buf, sem in (
        ("dp", N_DP, valid_src, valid_all, sem_valid), ("dp", N_DP, grad_src, grad_all, sem_grad),
        ("dp", N_DP, part_src, part_all, sem_part), ("dp", N_DP, stat_src, stat_all, sem_stat),
        ("rep", N_REP, step_src, step_all, sem_step), ("dp", N_DP, sums_src, sums_all, sem_sums),
    ):
        swap_wait(axis, size, src, buf, sem, False)


def hand_over(scal, *refs):
    n = (len(refs) - 3) // 2
    ins, (loss_out, valid_out), outs, sems = refs[:n], refs[n : n + 2], refs[n + 2 : -1], refs[-1]
    copies = [pltpu.make_async_copy(a, b, sems.at[i]) for i, (a, b) in enumerate(zip(ins, outs))]
    for c in copies:
        c.start()
    loss_out[0] = scal[0, 0]
    valid_out[0] = scal[1, 0]
    for c in copies:
        c.wait()


def shards(
    pixels, valid_mask, bottom_codes, top_codes, params, first_moment, second_moment, outer_momentum, ema_counts,
    ema_sums, codebooks, *, R,
):
    rows = pixels.shape[0]
    vm = pl.BlockSpec(memory_space=pltpu.VMEM)
    sm = pl.BlockSpec(memory_space=pltpu.SMEM)
    hbm = pl.BlockSpec(memory_space=pl.ANY)
    dma = pltpu.SemaphoreType.DMA
    results = [(SHARE, 128), (SHARE, 1, 128), (SHARE, 1, 128), (SHARE, 128), (1, 2, K), (1, 2, EMB, K), (1, 2, EMB, K)]
    inner = pl.pallas_call(
        functools.partial(kernel, R=R),
        out_shape=tuple(pltpu.VMEM(s, f32) for s in [(8, 128)] + results),
        in_specs=[hbm] * 2 + [vm] * 9,
        out_specs=(vm,) * 8,
        scratch_shapes=scratches(rows, R)
        + [
            pltpu.VMEM((rows, 384), f32), pltpu.VMEM((rows, 384), jnp.int32),
            pltpu.VMEM((8, 128), f32), pltpu.VMEM((N_DP, 8, 128), f32),
            pltpu.VMEM((16, 128), f32), pltpu.VMEM((N_DP, 16, 128), f32),
            pltpu.VMEM((N_DP, 48, 128), f32), pltpu.VMEM((N_DP, 48, 128), f32),
            pltpu.VMEM((N_DP, 8, 512), f32), pltpu.VMEM((N_DP, 8, 512), f32), pltpu.VMEM((N_DP, 8, 512), f32),
            pltpu.VMEM((N_REP, 48, 128), f32), pltpu.VMEM((N_DP, 48, 128), f32), dma((2,)),
        ]
        + [dma((N_DP,))] * 10 + [dma((N_REP,))] * 2,
        compiler_params=pltpu.CompilerParams(
            vmem_limit_bytes=60 * 2**20, collective_id=0, has_side_effects=True
        ),
    )(
        pixels, valid_mask, bottom_codes.reshape(-1, 128), top_codes.reshape(-1, 128), params,
        jnp.swapaxes(first_moment, 0, 1), jnp.swapaxes(second_moment, 0, 1), outer_momentum, ema_counts,
        jnp.swapaxes(ema_sums, 1, 2), jnp.swapaxes(codebooks, 1, 2),
    )
    shape = lambda *s: jax.ShapeDtypeStruct(s, f32)
    loss, valid, params, first, second, mom, counts, sums, books = pl.pallas_call(
        hand_over,
        out_shape=(shape(1), shape(1)) + tuple(shape(*s) for s in results),
        in_specs=[vm] * 8,
        out_specs=(sm, sm) + (hbm,) * 7,
        scratch_shapes=[dma((7,))],
    )(*(pltpu.with_memory_space_constraint(v, pltpu.VMEM) for v in inner))
    return (
        loss, valid, params, jnp.swapaxes(first, 0, 1), jnp.swapaxes(second, 0, 1), mom, counts,
        jnp.swapaxes(sums, 2, 3), jnp.swapaxes(books, 2, 3),
    )


def solution(mesh):
    return jax.shard_map(
        functools.partial(shards, R=256),
        mesh=mesh,
        in_specs=(
            P(("rep", "dp"), None),
            P(("rep", "dp"), None),
            P(("rep", "dp")),
            P(("rep", "dp")),
            P(),
            P("rep", "dp", None),
            P("rep", "dp", None),
            P("dp", None),
            P(),
            P(),
            P(),
        ),
        out_specs=(
            P("rep"),
            P("rep"),
            P("dp", None),
            P("rep", "dp", None),
            P("rep", "dp", None),
            P("dp", None),
            P("rep", None, None),
            P("rep", None, None, None),
            P("rep", None, None, None),
        ),
        check_vma=False,
    )
```

time: 70.4 us -> 44.5 us (0.63)
  the two profiles are of different devices: /device:TPU:0 before, /device:TPU:1 now
where the time goes in v1:
time: 44.5 us; the launch traced here: 44.3 us
  Pallas kernels  43.7 us (98%)
  between operations  0.65 us (1%)
    pallas_call x1, Pallas kernels, shards(): pl.pallas_call(functools.partial(kernel, R=R), out_shape=tuple((pltpu.VME...  42.3 us
    pallas_call x1, Pallas kernels, shards(): pl.pallas_call(hand_over, out_shape=(shape(1), shape(1)) + tuple((shape(*...  1.41 us

profile of v1, /device:TPU:1, one launch (start us, length us, event | category | flops | bytes accessed | tf_op | source)
XLA Modules:
  0.0 44.3 jit_solution(8492179884694760734)
XLA Ops:
  0.6 42.3 %shard_map.178 = (f32[8,128]{1,0:T(8,128)S(1)}, f32[46,128]{1,0:T(8,128)S(1)}, f32[46,1,128]{2,1,0:T(1,128)S(1)}, f32[46,1,128]{2,1,0:T(1,128)S(1)}, f32[46,128]...) custom-call(f32[1024,384]{1,0:T(8,128)} %x_hbm.1, ...), custom_call_target="tpu_custom_call" | custom-call | tf_op jit(solution)/shard_map/pallas_call | solution.py:553
  42.9 1.4 %shard_map.179 = (f32[1]{0:T(128)}, f32[1]{0:T(128)}, f32[46,128]{1,0:T(8,128)}, f32[46,1,128]{2,1,0:T(1,128)}, f32[46,1,128]{2,1,0:T(1,128)}, /*index=5*/f32[46...) custom-call(f32[8,128]{1,0:T(8,128)S(1)} %get-tuple-element.26.scal, ...), custom_call_target="tpu_custom_call" | custom-call | tf_op jit(solution)/shard_map/pallas_call | solution.py:577

commit v2 on v1

v2 whole, which is shorter than its diff:
```python
import functools
import jax
import jax.numpy as jnp
from jax import lax
from jax.experimental import pallas as pl
from jax.experimental.pallas import tpu as pltpu
from jax.sharding import PartitionSpec as P

PF = 48
EMB = 64
K = 512
STEP = 10
beta_commit = 0.25
ema_decay = 0.8
laplace_eps = 1e-05
inner_rate = 0.03
beta_first = 0.9
beta_second = 0.999
adam_eps = 1e-08
weight_decay = 0.01
outer_rate = 0.7
outer_moment = 0.9

bf16 = jnp.bfloat16
f32 = jnp.float32
O_ENC, O_RU, O_TI, O_DB, O_DT, O_RD, O_L, O_TO, O_OUT, O_END = 0, 48, 112, 368, 432, 496, 560, 624, 688, 736


def nn(a, b):
    return lax.dot_general(a, b, (((1,), (0,)), ((), ())), preferred_element_type=f32)


def nt(a, b):
    return lax.dot_general(a, b, (((1,), (1,)), ((), ())), preferred_element_type=f32)


def tn(a, b):
    return lax.dot_general(a, b, (((0,), (0,)), ((), ())), preferred_element_type=f32)


def split(v):
    hi = v.astype(bf16)
    return hi, (v - hi.astype(f32)).astype(bf16)


def pair(v):
    hi, lo = split(v)
    return jnp.concatenate([hi, lo], axis=1)


def quad(v):
    hi, lo = split(v)
    return jnp.concatenate([hi, hi, lo, lo], axis=1)


def twice(v):
    return jnp.concatenate([v, v], axis=0)


def silu_and_slope(u):
    w = 1.0 + jnp.tanh(u)
    a = u * w
    return a, w + a * (2.0 - w)


def lanes(parts):
    return jnp.concatenate(parts, axis=1)


def spread_codes(codes, per_row):
    a = codes.shape[0]
    rows = a * 128 // per_row
    span = 128 // per_row
    lo = (codes & 255).astype(f32).astype(bf16)
    hi = (codes >> 8).astype(f32).astype(bf16)
    up = (lax.broadcasted_iota(jnp.int32, (a, rows), 0) == lax.broadcasted_iota(jnp.int32, (a, rows), 1) // span)
    up = up.astype(f32).astype(bf16)
    keep = (
        lax.broadcasted_iota(jnp.int32, (128, rows), 0) // per_row
        == lax.broadcasted_iota(jnp.int32, (128, rows), 1) % span
    )
    pick = (
        lax.broadcasted_iota(jnp.int32, (8, 128), 0)
        == lax.broadcasted_iota(jnp.int32, (8, 128), 1) % per_row
    )
    pick = pick.astype(f32).astype(bf16)
    out = []
    for part in (lo, hi):
        wide = jnp.where(keep, tn(part, up), 0.0).astype(bf16)
        out.append(nn(pick, wide))
    return out


def stack(v):
    hi, lo = split(v)
    return jnp.concatenate([hi, lo], axis=0)


def halves(v):
    n = v.shape[0] // 2
    return v[:n] + v[n:]


def exact(a, b, dims):
    return lax.dot_general(a, b, ((dims), ((), ())), precision=lax.Precision.HIGHEST, preferred_element_type=f32)


WS = {
    "enc_f": (128, 96), "rd_f": (128, 128), "l_f": (128, 192), "ti_f": (128, 512), "to_f": (128, 128), "db_f": (128, 256),
    "dt_f": (128, 256), "out_f": (96, 128), "out_b": (128, 96), "db_b": (128, 128), "dt_b": (128, 128), "to_b": (128, 128),
    "ti_b": (256, 256), "ru_b": (64, 128), "he_b": (128, 256), "book_b": (256, 256), "book_t": (256, 256),
}
KEEP = {
    "x": (48, 8, f32), "xb": (48, 8, bf16), "he": (128, 8, bf16), "de": (128, 8, bf16), "ar": (64, 8, bf16), "dr": (64, 8, bf16),
    "gap_b": (64, 8, bf16), "gl": (64, 8, f32), "both": (128, 8, bf16),
}
KEEP_TOP = {
    "ti": (256, bf16), "ht": (128, bf16), "dt": (128, bf16), "gap_t": (64, f32), "gt": (64, f32),
}
ACC = {
    "e": (128, 48), "he": (128, 128), "ar": (64, 64), "ti": (256, 128), "to": (128, 64), "db": (128, 128), "dt": (128, 128),
    "out": (128, 48), "sum_b": (144, 256), "sum_t": (144, 256),
}


def weights(par, book_ref, w):
    part = par.T
    f = lambda lo, hi: par[lo:hi]
    t = lambda lo, hi: part[:, lo:hi]
    cross = exact(f(O_L, O_TO), f(O_RU, O_TI), ((1,), (1,)))
    w["enc_f"][...] = pair(0.5 * t(O_ENC, O_RU))
    w["rd_f"][...] = stack(0.5 * f(O_RD, O_L))
    w["l_f"][...] = stack(lanes([f(O_L, O_TO), cross]))
    w["ti_f"][...] = pair(0.5 * t(O_TI, O_DB))
    w["to_f"][...] = stack(f(O_TO, O_OUT))
    w["db_f"][...] = quad(0.5 * t(O_DB, O_DT))
    w["dt_f"][...] = quad(0.5 * t(O_DT, O_RD))
    w["out_f"][...] = stack(f(O_OUT, O_END))
    w["out_b"][...] = pair(0.5 * t(O_OUT, O_END))
    w["db_b"][...] = stack(f(O_DB, O_DT))
    w["dt_b"][...] = stack(f(O_DT, O_RD))
    w["to_b"][...] = pair(0.5 * t(O_TO, O_OUT))
    w["ti_b"][...] = pair(f(O_TI, O_DB))
    w["ru_b"][...] = pair(0.5 * exact(f(O_RU, O_TI), f(O_L, O_TO), ((1,), (1,))))
    w["he_b"][...] = pair(0.5 * lanes([t(O_L, O_TO), t(O_RD, O_L)]))
    for level, name in enumerate(("book_b", "book_t")):
        w[name][...] = jnp.concatenate([stack(book_ref[level][:, 256 * a : 256 * a + 256]) for a in (0, 1)], axis=0)


def code_keys(rows_ref, cols_ref, src, per):
    lo, hi = spread_codes(src[...], per)
    rows_ref[0] = lo
    rows_ref[1] = hi
    cols_ref[...] = lo.T


def high_bits(codes, level, n, at, R):
    return lanes([codes[level][0][1, p : p + 1, pl.ds(at, R)] for p in range(n)])


def first(i, size):
    return i * size if isinstance(i, int) else pl.multiple_of(i * size, size)


def hot(equal):
    return jnp.where(equal, jnp.ones((), bf16), jnp.zeros((), bf16))


def encoder(i, R, x_ref, codes, w, keep, acc):
    along = lax.broadcasted_iota(jnp.int32, (R, 256), 1).astype(f32).astype(bf16)
    at = first(i, R)
    tops = pl.ds(first(i, 2 * R), 2 * R)

    def scatter(level, n, latent):
        key = codes[level][1][pl.ds(at, R), :]
        low = jnp.concatenate([
            hot(along == jnp.broadcast_to(key[:, p : p + 1], (R, 256)).astype(bf16)) for p in range(n)
        ], axis=0)
        high = high_bits(codes, level, n, at, R).astype(bf16)
        ones = jnp.broadcast_to(high, latent.shape) * latent
        row = lax.broadcasted_iota(jnp.int32, (16, n * R), 0)
        count = jnp.where(row == 0, 1.0 - high.astype(f32), jnp.where(row == 1, high.astype(f32), 0.0)).astype(bf16)
        return nn(jnp.concatenate([latent - ones, ones, count], axis=0), low)

    xt = x_ref[pl.ds(at, R), :].T
    x = lanes([xt[48 * p : 48 * p + 48] for p in range(8)])
    keep["x"][i] = x
    xb = x.astype(bf16)
    keep["xb"][i] = xb
    he, de = silu_and_slope(nn(w["enc_f"][...], twice(xb)))
    heb = he.astype(bf16)
    keep["he"][i] = heb
    keep["de"][i] = de.astype(bf16)
    ar, dr = silu_and_slope(halves(nn(w["rd_f"][...], heb)))
    arb = ar.astype(bf16)
    keep["ar"][i] = arb
    keep["dr"][i] = dr.astype(bf16)
    lbb = halves(nn(w["l_f"][...], jnp.concatenate([heb, arb], axis=0))).astype(bf16)
    ti = lanes([
        jnp.concatenate([lbb[:, R * p : R * p + R] for p in range(4 * g, 4 * g + 4)], axis=0) for g in (0, 1)
    ])
    keep["ti"][:, tops] = ti
    ht, dt = silu_and_slope(nn(w["ti_f"][...], twice(ti)))
    htb = ht.astype(bf16)
    keep["ht"][:, tops] = htb
    keep["dt"][:, tops] = dt.astype(bf16)
    lt = halves(nn(w["to_f"][...], htb))
    keep["gap_t"][:, tops] = lt
    acc["sum_b"][...] += scatter(0, 8, lbb)
    acc["sum_t"][...] += scatter(1, 2, lt.astype(bf16))


def decoder(i, R, m_ref, codes, w, keep, acc, lacc):
    down = lax.broadcasted_iota(jnp.int32, (256, R), 0).astype(f32).astype(bf16)
    at = first(i, R)
    tops = pl.ds(first(i, 2 * R), 2 * R)

    def gather(level, n, book):
        key = codes[level][0][0, :, pl.ds(at, R)]
        low = lanes([hot(down == key[p : p + 1, :].astype(bf16)) for p in range(n)])
        both = nn(book, low)
        return jnp.where(high_bits(codes, level, n, at, R) > 0.5, both[128:], both[:128]).astype(bf16)

    mt = m_ref[pl.ds(at, R), :].astype(f32).T
    m = lanes([mt[48 * p : 48 * p + 48] for p in range(8)])
    qb2 = gather(0, 8, w["book_b"][...])
    qt2 = gather(1, 2, w["book_t"][...])
    ti = keep["ti"][:, tops]
    lb = lanes([ti[64 * (p % 4) : 64 * (p % 4) + 64, R * (p // 4) : R * (p // 4) + R] for p in range(8)]).astype(f32)
    gap_b = lb - halves(qb2.astype(f32))
    gap_t = keep["gap_t"][:, tops] - halves(qt2.astype(f32))
    keep["gap_b"][i] = gap_b.astype(bf16)
    keep["gap_t"][:, tops] = gap_t
    top = nn(w["dt_f"][...], twice(qt2))
    pre = nn(w["db_f"][...], twice(qb2)) + lanes([top[:, R * (p // 4) : R * (p // 4) + R] for p in range(8)])
    hd, dd = silu_and_slope(pre)
    hdb = hd.astype(bf16)
    err = halves(nn(w["out_f"][...], hdb)) - keep["x"][i]
    me = m * err
    lacc[0:48] += sum((me * err)[:, R * p : R * p + R] for p in range(8))
    lacc[48:112] += sum((gap_b * gap_b)[:, R * p : R * p + R] for p in range(8))
    lacc[112:176] += sum((gap_t * gap_t)[:, R * p : R * p + R] for p in range(2))
    grb = me.astype(bf16)
    acc["out"][...] += nt(hdb, grb)
    gpd = nn(w["out_b"][...], twice(grb)) * dd
    gpdb = gpd.astype(bf16)
    acc["db"][...] += nt(qb2, gpdb)
    gtrb = lanes([sum(gpd[:, R * p : R * p + R] for p in range(4 * g_, 4 * g_ + 4)) for g_ in (0, 1)]).astype(bf16)
    acc["dt"][...] += nt(qt2, gtrb)
    keep["gt"][:, tops] = halves(nn(w["dt_b"][...], gtrb))
    keep["gl"][i] = halves(nn(w["db_b"][...], gpdb))


def top_backward(n, R, kt, w, keep, acc):
    gltb = (keep["gt"][...] + kt * keep["gap_t"][...]).astype(bf16)
    acc["to"][...] = nt(keep["ht"][...], gltb)
    gptb = (nn(w["to_b"][...], twice(gltb)) * keep["dt"][...].astype(f32)).astype(bf16)
    acc["ti"][...] = nt(keep["ti"][...], gptb)
    gti = nn(w["ti_b"][...], twice(gptb))
    for i in range(n):
        for p in range(8):
            at = 2 * R * i + R * (p // 4)
            keep["gl"][i, :, R * p : R * p + R] += gti[64 * (p % 4) : 64 * (p % 4) + 64, at : at + R]


def backward_inner(i, kb, w, keep, acc):
    glbb = (keep["gl"][i] + kb * keep["gap_b"][i].astype(f32)).astype(bf16)
    gprb = (nn(w["ru_b"][...], twice(glbb)) * keep["dr"][i].astype(f32)).astype(bf16)
    both = jnp.concatenate([glbb, gprb], axis=0)
    keep["both"][i] = both
    acc["he"][...] += nt(both, keep["he"][i])
    acc["ar"][...] += nt(glbb, keep["ar"][i])


def backward_outer(i, w, keep, acc):
    gpeb = (nn(w["he_b"][...], twice(keep["both"][i])) * keep["de"][i].astype(f32)).astype(bf16)
    acc["e"][...] += nt(gpeb, keep["xb"][i])


def scratches(rows, R):
    return (
        [pltpu.VMEM(s, bf16) for s in WS.values()]
        + [pltpu.VMEM((rows // R, c, n * R), t) for c, n, t in KEEP.values()]
        + [pltpu.VMEM((c, rows * 2), t) for c, t in KEEP_TOP.values()]
        + [pltpu.VMEM(s, f32) for s in ACC.values()]
        + [pltpu.VMEM((2, 8, rows), f32), pltpu.VMEM((rows, 8), f32)] * 2
        + [pltpu.VMEM((176, R), f32)]
    )


def unscratch(scratch):
    scratch = list(scratch)
    take = lambda names: {k: scratch.pop(0) for k in names}
    w, keep, acc = take(WS), take(list(KEEP) + list(KEEP_TOP)), take(ACC)
    codes = ((scratch.pop(0), scratch.pop(0)), (scratch.pop(0), scratch.pop(0)))
    return w, keep, acc, codes, scratch


def swap_start(axis, n, src_at, buf, sems):
    me = lax.axis_index(axis)

    def go(k, carry):
        peer = lax.rem(me + k, n)
        pltpu.make_async_remote_copy(
            src_ref=src_at(peer), dst_ref=buf.at[me], send_sem=sems[0], recv_sem=sems[1],
            device_id={axis: peer}, device_id_type=pl.DeviceIdType.MESH,
        ).start()
        return carry

    lax.fori_loop(1, n, go, 0)


def swap_wait(axis, n, buf, sems, recv):
    others = buf.at[0 : n - 1]
    copy = pltpu.make_async_remote_copy(
        src_ref=others, dst_ref=others, send_sem=sems[0], recv_sem=sems[1],
        device_id={axis: lax.axis_index(axis)}, device_id_type=pl.DeviceIdType.MESH,
    )
    if recv:
        copy.wait_recv()
    else:
        copy.wait_send()


def total(v):
    return jnp.sum(jnp.sum(v, axis=0, keepdims=True), axis=1, keepdims=True)


def in_order(buf, n):
    out = buf[0]
    for s in range(1, n):
        out = out + buf[s]
    return out

N_DP = 16
N_REP = 8
SHARE = 46
AFTER_DECODER = (8, 9, 15)
AFTER_TOP = (3, 4, 5, 6, 7, 14)
AFTER_INNER = (2, 10, 11, 12, 13)
AFTER_OUTER = (0, 1)


def share_start(shares, src, buf, sems):
    me = lax.axis_index("dp")
    for s in shares:
        @pl.when(me != s)
        def _():
            pltpu.make_async_remote_copy(
                src_ref=src.at[s], dst_ref=buf.at[me], send_sem=sems[0], recv_sem=sems[1],
                device_id={"dp": s}, device_id_type=pl.DeviceIdType.MESH,
            ).start()


def put_rows(ref, at, v):
    end = at + v.shape[0]
    for s in range(N_DP):
        lo, hi = max(at, SHARE * s), min(end, SHARE * s + SHARE)
        if lo < hi:
            ref[s, lo - SHARE * s : hi - SHARE * s] = v[lo - at : hi - at]


def each(n, f):
    if n == 1:
        f(0)
        return

    def go(i, carry):
        f(i)
        return carry

    lax.fori_loop(0, n, go, 0)


def kernel(*refs, R):
    sources, refs = refs[:11], refs[11:]
    (scal_out, params_out, first_out, second_out, mom_out, counts_out, sums_out, books_out), scratch = refs[:8], refs[8:]
    inputs, scratch = scratch[:11], scratch[11:]
    x_ref, m_ref, cb_ref, ct_ref, p_ref, first_ref, second_ref, mom_ref, cnt_ref, ema_ref, book_ref = inputs
    w, keep, acc, codes, scratch = unscratch(scratch)
    (
        lacc, valid_own, valid_all, stat_own, stat_all, grad_own, grad_all, part_own, part_all, sums_all, step_all,
        par_share, in_sems, *sems,
    ) = scratch
    loads = [pltpu.make_async_copy(a, b, in_sems.at[i]) for i, (a, b) in enumerate(zip(sources, inputs))]
    load_x, load_m, load_cb, load_ct, load_p, *load_rest, load_book = loads
    for load in (load_p, load_x, load_cb, load_ct, load_book, load_m, *load_rest):
        load.start()
    sems = [(sems[2 * i], sems[2 * i + 1]) for i in range(6)]
    sem_valid, sem_stat, sem_grad, sem_part, sem_sums, sem_step = sems
    dp = lax.axis_index("dp")
    rep = lax.axis_index("rep")
    rows = x_ref.shape[0]
    n = rows // R

    barrier = pltpu.get_barrier_semaphore()
    for axis, size, me in (("dp", N_DP, dp), ("rep", N_REP, rep)):
        def hello(k, carry):
            pl.semaphore_signal(
                barrier, inc=1, device_id={axis: lax.rem(me + k, size)}, device_id_type=pl.DeviceIdType.MESH
            )
            return carry

        lax.fori_loop(1, size, hello, 0)

    for load in (load_p, load_x, load_cb, load_ct, load_book):
        load.wait()
    weights(p_ref[...], book_ref, w)
    code_keys(*codes[0], cb_ref, 8)
    code_keys(*codes[1], ct_ref, 2)
    for v in acc.values():
        v[...] = jnp.zeros_like(v)
    lacc[...] = jnp.zeros_like(lacc)
    for s in range(N_DP):
        par_share[s, 0:SHARE] = p_ref[SHARE * s : SHARE * s + SHARE]
        grad_own[s] = jnp.zeros((48, 128), f32)
    each(n, lambda i: encoder(i, R, x_ref, codes, w, keep, acc))

    load_m.wait()
    valid_own[...] = jnp.broadcast_to(total(m_ref[...].astype(f32)), (8, 128))
    valid_all[dp] = valid_own[...]
    valid_src = lambda peer: valid_own
    pl.semaphore_wait(barrier, N_DP + N_REP - 2)
    swap_start("dp", N_DP, valid_src, valid_all, sem_valid)

    for d in range(N_DP):
        name, at = ("sum_b", "sum_t")[d // 8], 8 * (d % 8)
        part_own[d] = lanes([acc[name][at : at + 8], acc[name][64 + at : 72 + at]])
    part_src = lambda peer: part_own.at[peer]
    swap_start("dp", N_DP, part_src, part_all, sem_part)
    stat_own[...] = jnp.concatenate(
        [
            acc[name][128 + a : 129 + a, 128 * j : 128 * j + 128]
            for name in ("sum_b", "sum_t") for a in (0, 1) for j in (0, 1)
        ], axis=0
    )
    stat_src = lambda peer: stat_own
    swap_start("dp", N_DP, stat_src, stat_all, sem_stat)
    part_all[dp] = part_own[dp]
    stat_all[dp] = stat_own[...]

    each(n, lambda i: decoder(i, R, m_ref, codes, w, keep, acc, lacc))

    group_rows = rows * 8 * N_DP
    swap_wait("dp", N_DP, valid_all, sem_valid, True)
    count = in_order(valid_all, N_DP)[0:1, 0:1]
    scale = 2.0 / count
    kb = beta_commit / (group_rows * EMB) * count
    kt = beta_commit / (group_rows // 4 * EMB) * count
    lane = lax.broadcasted_iota(jnp.int32, (1, 128), 1)
    losses = jnp.where(lane == 0, total(lacc[0:48]), jnp.where(lane == 1, total(lacc[48:112]), total(lacc[112:176])))
    for s in range(N_DP):
        grad_own[s, SHARE : SHARE + 1] = losses
    put_rows(grad_own, O_DB, halves(acc["db"][...]) * scale)
    put_rows(grad_own, O_DT, halves(acc["dt"][...]) * scale)
    put_rows(grad_own, O_OUT, acc["out"][...].T * scale)
    share_start(AFTER_DECODER, grad_own, grad_all, sem_grad)

    top_backward(n, R, kt, w, keep, acc)
    put_rows(grad_own, O_TI, acc["ti"][...] * scale)
    put_rows(grad_own, O_TO, acc["to"][...].T * scale)
    share_start(AFTER_TOP, grad_own, grad_all, sem_grad)

    each(n, lambda i: backward_inner(i, kb, w, keep, acc))
    cross = acc["ar"][...]
    put_rows(grad_own, O_RU, exact(cross, p_ref[O_L:O_TO], ((0,), (0,))) * scale)
    put_rows(grad_own, O_RD, acc["he"][64:128] * scale)
    put_rows(grad_own, O_L, (acc["he"][0:64] + exact(cross, p_ref[O_RU:O_TI], ((1,), (0,)))) * scale)
    share_start(AFTER_INNER, grad_own, grad_all, sem_grad)

    each(n, lambda i: backward_outer(i, w, keep, acc))
    put_rows(grad_own, O_ENC, acc["e"][...].T * scale)
    share_start(AFTER_OUTER, grad_own, grad_all, sem_grad)
    grad_all[dp] = grad_own[dp]

    for load in load_rest:
        load.wait()
    swap_wait("dp", N_DP, grad_all, sem_grad, True)
    summed = in_order(grad_all, N_DP)
    grads = summed[0:SHARE]
    own = par_share[dp][0:SHARE]
    first_new = beta_first * first_ref[:, 0, :] + (1.0 - beta_first) * grads
    second_new = beta_second * second_ref[:, 0, :] + (1.0 - beta_second) * grads * grads
    bias_first = 1.0 - beta_first**STEP
    bias_second = 1.0 - beta_second**STEP
    step_here = inner_rate * (
        first_new / bias_first / (jnp.sqrt(second_new / bias_second) + adam_eps) + weight_decay * own
    )
    step_all[rep, 0:SHARE] = step_here
    step_all[rep, SHARE:48] = jnp.zeros((48 - SHARE, 128), f32)
    step_src = lambda peer: step_all.at[rep]
    swap_start("rep", N_REP, step_src, step_all, sem_step)
    swap_wait("dp", N_DP, part_all, sem_part, True)
    sums_all[dp] = in_order(part_all, N_DP)
    sums_src = lambda peer: sums_all.at[dp]
    swap_start("dp", N_DP, sums_src, sums_all, sem_sums)

    first_out[:, 0, :] = first_new
    second_out[:, 0, :] = second_new

    swap_wait("dp", N_DP, stat_all, sem_stat, True)
    stats = in_order(stat_all, N_DP)
    seen = jnp.concatenate([lanes([stats[4 * level + j : 4 * level + j + 1] for j in range(4)]) for level in (0, 1)], axis=0)
    counts_new = ema_decay * cnt_ref[...] + (1.0 - ema_decay) * seen
    counts_out[0] = counts_new
    totals = jnp.sum(counts_new, axis=1, keepdims=True)
    smooth = (counts_new + laplace_eps) / (totals + K * laplace_eps) * totals
    terms = summed[SHARE : SHARE + 1]
    loss = terms[:, 0:1] / count + beta_commit * (
        terms[:, 1:2] / (group_rows * EMB) + terms[:, 2:3] / (group_rows // 4 * EMB)
    )
    scal_out[...] = jnp.concatenate([jnp.broadcast_to(loss, (1, 128)), jnp.broadcast_to(count, (1, 128)), jnp.zeros((6, 128), f32)], axis=0)

    swap_wait("dp", N_DP, sums_all, sem_sums, True)
    for level in (0, 1):
        inverse = 1.0 / smooth[level : level + 1]
        for j in range(8):
            rows_j = slice(8 * j, 8 * j + 8)
            sums_new = ema_decay * ema_ref[level, rows_j] + (1.0 - ema_decay) * sums_all[8 * level + j]
            sums_out[0, level, rows_j] = sums_new
            books_out[0, level, rows_j] = sums_new * inverse

    swap_wait("rep", N_REP, step_all, sem_step, True)
    mean_delta = in_order(step_all, N_REP)[0:SHARE] * (1.0 / N_REP)
    momentum_new = outer_moment * mom_ref[...] + mean_delta
    mom_out[...] = momentum_new
    params_out[...] = own - outer_rate * (mean_delta + outer_moment * momentum_new)

    for axis, size, buf, sem in (
        ("dp", N_DP, valid_all, sem_valid), ("dp", N_DP, grad_all, sem_grad), ("dp", N_DP, part_all, sem_part),
        ("dp", N_DP, stat_all, sem_stat), ("rep", N_REP, step_all, sem_step), ("dp", N_DP, sums_all, sem_sums),
    ):
        swap_wait(axis, size, buf, sem, False)


def hand_over(scal, *refs):
    n = (len(refs) - 3) // 2
    ins, (loss_out, valid_out), outs, sems = refs[:n], refs[n : n + 2], refs[n + 2 : -1], refs[-1]
    copies = [pltpu.make_async_copy(a, b, sems.at[i]) for i, (a, b) in enumerate(zip(ins, outs))]
    for c in copies:
        c.start()
    loss_out[0] = scal[0, 0]
    valid_out[0] = scal[1, 0]
    for c in copies:
        c.wait()


def shards(
    pixels, valid_mask, bottom_codes, top_codes, params, first_moment, second_moment, outer_momentum, ema_counts,
    ema_sums, codebooks, *, R,
):
    rows = pixels.shape[0]
    vm = pl.BlockSpec(memory_space=pltpu.VMEM)
    sm = pl.BlockSpec(memory_space=pltpu.SMEM)
    hbm = pl.BlockSpec(memory_space=pl.ANY)
    dma = pltpu.SemaphoreType.DMA
    args = (
        pixels, valid_mask, bottom_codes.reshape(-1, 128), top_codes.reshape(-1, 128), params,
        jnp.swapaxes(first_moment, 0, 1), jnp.swapaxes(second_moment, 0, 1), outer_momentum, ema_counts,
        jnp.swapaxes(ema_sums, 1, 2), jnp.swapaxes(codebooks, 1, 2),
    )
    results = [(SHARE, 128), (SHARE, 1, 128), (SHARE, 1, 128), (SHARE, 128), (1, 2, K), (1, 2, EMB, K), (1, 2, EMB, K)]
    inner = pl.pallas_call(
        functools.partial(kernel, R=R),
        out_shape=tuple(pltpu.VMEM(s, f32) for s in [(8, 128)] + results),
        in_specs=[hbm] * 11,
        out_specs=(vm,) * 8,
        scratch_shapes=[pltpu.VMEM(v.shape, v.dtype) for v in args]
        + scratches(rows, R)
        + [
            pltpu.VMEM((8, 128), f32), pltpu.VMEM((N_DP, 8, 128), f32),
            pltpu.VMEM((8, 128), f32), pltpu.VMEM((N_DP, 8, 128), f32),
            pltpu.VMEM((N_DP, 48, 128), f32), pltpu.VMEM((N_DP, 48, 128), f32),
            pltpu.VMEM((N_DP, 8, 512), f32), pltpu.VMEM((N_DP, 8, 512), f32), pltpu.VMEM((N_DP, 8, 512), f32),
            pltpu.VMEM((N_REP, 48, 128), f32), pltpu.VMEM((N_DP, 48, 128), f32), dma((11,)),
        ]
        + [dma] * 12,
        compiler_params=pltpu.CompilerParams(
            vmem_limit_bytes=60 * 2**20, collective_id=0, has_side_effects=True
        ),
    )(*args)
    shape = lambda *s: jax.ShapeDtypeStruct(s, f32)
    loss, valid, params, first, second, mom, counts, sums, books = pl.pallas_call(
        hand_over,
        out_shape=(shape(1), shape(1)) + tuple(shape(*s) for s in results),
        in_specs=[vm] * 8,
        out_specs=(sm, sm) + (hbm,) * 7,
        scratch_shapes=[dma((7,))],
    )(*(pltpu.with_memory_space_constraint(v, pltpu.VMEM) for v in inner))
    return (
        loss, valid, params, jnp.swapaxes(first, 0, 1), jnp.swapaxes(second, 0, 1), mom, counts,
        jnp.swapaxes(sums, 2, 3), jnp.swapaxes(books, 2, 3),
    )


def solution(mesh):
    return jax.shard_map(
        functools.partial(shards, R=1024),
        mesh=mesh,
        in_specs=(
            P(("rep", "dp"), None),
            P(("rep", "dp"), None),
            P(("rep", "dp")),
            P(("rep", "dp")),
            P(),
            P("rep", "dp", None),
            P("rep", "dp", None),
            P("dp", None),
            P(),
            P(),
            P(),
        ),
        out_specs=(
            P("rep"),
            P("rep"),
            P("dp", None),
            P("rep", "dp", None),
            P("rep", "dp", None),
            P("dp", None),
            P("rep", None, None),
            P("rep", None, None, None),
            P("rep", None, None, None),
        ),
        check_vma=False,
    )
```

time: 44.5 us -> 39.2 us (0.88)
  Pallas kernels: 43.7 us -> 38.3 us
    pallas_call x1, Pallas kernels: 42.3 us -> 36.9 us  [shards(): pl.pallas_call(functools.partial(kernel, R=R), out_shape=tuple((pltpu.VME...]
where the time goes in v2:
time: 39.2 us; the launch traced here: 39.1 us
  Pallas kernels  38.3 us (98%)
  between operations  0.81 us (2%)
    pallas_call x1, Pallas kernels, shards(): pl.pallas_call(functools.partial(kernel, R=R), out_shape=tuple((pltpu.VME...  36.9 us
    pallas_call x1, Pallas kernels, shards(): pl.pallas_call(hand_over, out_shape=(shape(1), shape(1)) + tuple((shape(*...  1.41 us

profile of v2, /device:TPU:1, one launch (start us, length us, event | category | flops | bytes accessed | tf_op | source)
XLA Modules:
  0.0 39.1 jit_solution(9090357867739472964)
XLA Ops:
  0.6 36.9 %shard_map.178 = (f32[8,128]{1,0:T(8,128)S(1)}, f32[46,128]{1,0:T(8,128)S(1)}, f32[46,1,128]{2,1,0:T(1,128)S(1)}, f32[46,1,128]{2,1,0:T(1,128)S(1)}, f32[46,128]...) custom-call(f32[1024,384]{1,0:T(8,128)} %refs_0_.1, ...), custom_call_target="tpu_custom_call" | custom-call | tf_op jit(solution)/shard_map/pallas_call | solution.py:563
  37.5 1.4 %shard_map.179 = (f32[1]{0:T(128)}, f32[1]{0:T(128)}, f32[46,128]{1,0:T(8,128)}, f32[46,1,128]{2,1,0:T(1,128)}, f32[46,1,128]{2,1,0:T(1,128)}, /*index=5*/f32[46...) custom-call(f32[8,128]{1,0:T(8,128)S(1)} %get-tuple-element.26.scal, ...), custom_call_target="tpu_custom_call" | custom-call | tf_op jit(solution)/shard_map/pallas_call | solution.py:583

commit v3 on v2

--- a/solution.py
+++ b/solution.py
@@ -112,14 +112,15 @@
 }
 KEEP = {
     "x": (48, 8, f32), "xb": (48, 8, bf16), "he": (128, 8, bf16), "de": (128, 8, bf16), "ar": (64, 8, bf16), "dr": (64, 8, bf16),
-    "gap_b": (64, 8, bf16), "gl": (64, 8, f32), "both": (128, 8, bf16),
+    "gap_b": (64, 8, bf16), "gl": (64, 8, f32), "both": (128, 8, bf16), "hd": (128, 8, bf16), "gr": (48, 8, bf16),
+    "gpd": (128, 8, bf16), "qb": (128, 8, bf16),
 }
 KEEP_TOP = {
-    "ti": (256, bf16), "ht": (128, bf16), "dt": (128, bf16), "gap_t": (64, f32), "gt": (64, f32),
+    "ti": (256, bf16), "ht": (128, bf16), "dt": (128, bf16), "gap_t": (64, f32), "gt": (64, f32), "qt": (128, bf16), "gtr": (128, bf16),
+    "glt": (64, bf16), "gpt": (128, bf16),
 }
 ACC = {
-    "e": (128, 48), "he": (128, 128), "ar": (64, 64), "ti": (256, 128), "to": (128, 64), "db": (128, 128), "dt": (128, 128),
-    "out": (128, 48), "sum_b": (144, 256), "sum_t": (144, 256),
+    "e": (128, 48), "he": (128, 128), "ar": (64, 64), "db": (128, 128), "out": (128, 48), "sum_b": (144, 256), "sum_t": (144, 256),
 }
 
 
@@ -241,21 +242,24 @@
     lacc[48:112] += sum((gap_b * gap_b)[:, R * p : R * p + R] for p in range(8))
     lacc[112:176] += sum((gap_t * gap_t)[:, R * p : R * p + R] for p in range(2))
     grb = me.astype(bf16)
-    acc["out"][...] += nt(hdb, grb)
     gpd = nn(w["out_b"][...], twice(grb)) * dd
     gpdb = gpd.astype(bf16)
-    acc["db"][...] += nt(qb2, gpdb)
     gtrb = lanes([sum(gpd[:, R * p : R * p + R] for p in range(4 * g_, 4 * g_ + 4)) for g_ in (0, 1)]).astype(bf16)
-    acc["dt"][...] += nt(qt2, gtrb)
     keep["gt"][:, tops] = halves(nn(w["dt_b"][...], gtrb))
     keep["gl"][i] = halves(nn(w["db_b"][...], gpdb))
-
-
-def top_backward(n, R, kt, w, keep, acc):
+    keep["hd"][i] = hdb
+    keep["gr"][i] = grb
+    keep["gpd"][i] = gpdb
+    keep["qb"][i] = qb2
+    keep["qt"][:, tops] = qt2
+    keep["gtr"][:, tops] = gtrb
+
+
+def top_backward(n, R, kt, w, keep):
     gltb = (keep["gt"][...] + kt * keep["gap_t"][...]).astype(bf16)
-    acc["to"][...] = nt(keep["ht"][...], gltb)
+    keep["glt"][...] = gltb
     gptb = (nn(w["to_b"][...], twice(gltb)) * keep["dt"][...].astype(f32)).astype(bf16)
-    acc["ti"][...] = nt(keep["ti"][...], gptb)
+    keep["gpt"][...] = gptb
     gti = nn(w["ti_b"][...], twice(gptb))
     for i in range(n):
         for p in range(8):
@@ -268,13 +272,16 @@
     gprb = (nn(w["ru_b"][...], twice(glbb)) * keep["dr"][i].astype(f32)).astype(bf16)
     both = jnp.concatenate([glbb, gprb], axis=0)
     keep["both"][i] = both
-    acc["he"][...] += nt(both, keep["he"][i])
     acc["ar"][...] += nt(glbb, keep["ar"][i])
 
 
 def backward_outer(i, w, keep, acc):
     gpeb = (nn(w["he_b"][...], twice(keep["both"][i])) * keep["de"][i].astype(f32)).astype(bf16)
     acc["e"][...] += nt(gpeb, keep["xb"][i])
+
+
+def add(ref, v):
+    ref[...] += v
 
 
 def scratches(rows, R):
@@ -335,12 +342,6 @@
 N_DP = 16
 N_REP = 8
 SHARE = 46
-AFTER_DECODER = (8, 9, 15)
-AFTER_TOP = (3, 4, 5, 6, 7, 14)
-AFTER_INNER = (2, 10, 11, 12, 13)
-AFTER_OUTER = (0, 1)
-
-
 def share_start(shares, src, buf, sems):
     me = lax.axis_index("dp")
     for s in shares:
@@ -403,7 +404,7 @@
 
         lax.fori_loop(1, size, hello, 0)
 
-    for load in (load_p, load_x, load_cb, load_ct, load_book):
+    for load in (load_p, load_book, load_cb, load_ct):
         load.wait()
     weights(p_ref[...], book_ref, w)
     code_keys(*codes[0], cb_ref, 8)
@@ -411,9 +412,7 @@
     for v in acc.values():
         v[...] = jnp.zeros_like(v)
     lacc[...] = jnp.zeros_like(lacc)
-    for s in range(N_DP):
-        par_share[s, 0:SHARE] = p_ref[SHARE * s : SHARE * s + SHARE]
-        grad_own[s] = jnp.zeros((48, 128), f32)
+    load_x.wait()
     each(n, lambda i: encoder(i, R, x_ref, codes, w, keep, acc))
 
     load_m.wait()
@@ -450,31 +449,43 @@
     lane = lax.broadcasted_iota(jnp.int32, (1, 128), 1)
     losses = jnp.where(lane == 0, total(lacc[0:48]), jnp.where(lane == 1, total(lacc[48:112]), total(lacc[112:176])))
     for s in range(N_DP):
-        grad_own[s, SHARE : SHARE + 1] = losses
+        grad_own[s, SHARE:48] = jnp.broadcast_to(losses, (48 - SHARE, 128))
+    top_backward(n, R, kt, w, keep)
+    each(n, lambda i: backward_inner(i, kb, w, keep, acc))
+    each(n, lambda i: backward_outer(i, w, keep, acc))
+    cross = acc["ar"][...]
+    put_rows(grad_own, O_ENC, acc["e"][...].T * scale)
+    put_rows(grad_own, O_RU, exact(cross, p_ref[O_L:O_TO], ((0,), (0,))) * scale)
+    share_start((0, 1), grad_own, grad_all, sem_grad)
+    put_rows(grad_own, O_TI, nt(keep["ti"][...], keep["gpt"][...]) * scale)
+    share_start((2, 3, 4, 5, 6, 7), grad_own, grad_all, sem_grad)
+    each(n, lambda i: add(acc["db"], nt(keep["qb"][i], keep["gpd"][i])))
     put_rows(grad_own, O_DB, halves(acc["db"][...]) * scale)
-    put_rows(grad_own, O_DT, halves(acc["dt"][...]) * scale)
-    put_rows(grad_own, O_OUT, acc["out"][...].T * scale)
-    share_start(AFTER_DECODER, grad_own, grad_all, sem_grad)
-
-    top_backward(n, R, kt, w, keep, acc)
-    put_rows(grad_own, O_TI, acc["ti"][...] * scale)
-    put_rows(grad_own, O_TO, acc["to"][...].T * scale)
-    share_start(AFTER_TOP, grad_own, grad_all, sem_grad)
-
-    each(n, lambda i: backward_inner(i, kb, w, keep, acc))
-    cross = acc["ar"][...]
-    put_rows(grad_own, O_RU, exact(cross, p_ref[O_L:O_TO], ((0,), (0,))) * scale)
+    put_rows(grad_own, O_DT, halves(nt(keep["qt"][...], keep["gtr"][...])) * scale)
+    share_start((8, 9), grad_own, grad_all, sem_grad)
+    each(n, lambda i: add(acc["he"], nt(keep["both"][i], keep["he"][i])))
     put_rows(grad_own, O_RD, acc["he"][64:128] * scale)
     put_rows(grad_own, O_L, (acc["he"][0:64] + exact(cross, p_ref[O_RU:O_TI], ((1,), (0,)))) * scale)
-    share_start(AFTER_INNER, grad_own, grad_all, sem_grad)
-
-    each(n, lambda i: backward_outer(i, w, keep, acc))
-    put_rows(grad_own, O_ENC, acc["e"][...].T * scale)
-    share_start(AFTER_OUTER, grad_own, grad_all, sem_grad)
+    put_rows(grad_own, O_TO, nt(keep["ht"][...], keep["glt"][...]).T * scale)
+    share_start((12, 13, 10, 11), grad_own, grad_all, sem_grad)
+    each(n, lambda i: add(acc["out"], nt(keep["hd"][i], keep["gr"][i])))
+    put_rows(grad_own, O_OUT, acc["out"][...].T * scale)
+    share_start((14, 15), grad_own, grad_all, sem_grad)
     grad_all[dp] = grad_own[dp]
 
     for load in load_rest:
         load.wait()
+    for s in range(N_DP):
+        par_share[s, 0:SHARE] = p_ref[SHARE * s : SHARE * s + SHARE]
+    swap_wait("dp", N_DP, part_all, sem_part, True)
+    sums_all[dp] = in_order(part_all, N_DP)
+    swap_wait("dp", N_DP, stat_all, sem_stat, True)
+    stats = in_order(stat_all, N_DP)
+    seen = jnp.concatenate([lanes([stats[4 * level + j : 4 * level + j + 1] for j in range(4)]) for level in (0, 1)], axis=0)
+    counts_new = ema_decay * cnt_ref[...] + (1.0 - ema_decay) * seen
+    counts_out[0] = counts_new
+    totals = jnp.sum(counts_new, axis=1, keepdims=True)
+    smooth = (counts_new + laplace_eps) / (totals + K * laplace_eps) * totals
     swap_wait("dp", N_DP, grad_all, sem_grad, True)
     summed = in_order(grad_all, N_DP)
     grads = summed[0:SHARE]
@@ -490,21 +501,12 @@
     step_all[rep, SHARE:48] = jnp.zeros((48 - SHARE, 128), f32)
     step_src = lambda peer: step_all.at[rep]
     swap_start("rep", N_REP, step_src, step_all, sem_step)
-    swap_wait("dp", N_DP, part_all, sem_part, True)
-    sums_all[dp] = in_order(part_all, N_DP)
     sums_src = lambda peer: sums_all.at[dp]
     swap_start("dp", N_DP, sums_src, sums_all, sem_sums)
 
     first_out[:, 0, :] = first_new
     second_out[:, 0, :] = second_new
 
-    swap_wait("dp", N_DP, stat_all, sem_stat, True)
-    stats = in_order(stat_all, N_DP)
-    seen = jnp.concatenate([lanes([stats[4 * level + j : 4 * level + j + 1] for j in range(4)]) for level in (0, 1)], axis=0)
-    counts_new = ema_decay * cnt_ref[...] + (1.0 - ema_decay) * seen
-    counts_out[0] = counts_new
-    totals = jnp.sum(counts_new, axis=1, keepdims=True)
-    smooth = (counts_new + laplace_eps) / (totals + K * laplace_eps) * totals
     terms = summed[SHARE : SHARE + 1]
     loss = terms[:, 0:1] / count + beta_commit * (
         terms[:, 1:2] / (group_rows * EMB) + terms[:, 2:3] / (group_rows // 4 * EMB)

time: 39.2 us -> 36.2 us (0.923)
  the two profiles are of different devices: /device:TPU:1 before, /device:TPU:0 now
where the time goes in v3:
time: 36.2 us; the launch traced here: 36.1 us
  Pallas kernels  35.2 us (97%)
  between operations  0.81 us (2%)
    pallas_call x1, Pallas kernels, shards(): pl.pallas_call(functools.partial(kernel, R=R), out_shape=tuple((pltpu.VME...  33.8 us
    pallas_call x1, Pallas kernels, shards(): pl.pallas_call(hand_over, out_shape=(shape(1), shape(1)) + tuple((shape(*...  1.41 us

profile of v3, /device:TPU:0, one launch (start us, length us, event | category | flops | bytes accessed | tf_op | source)
XLA Modules:
  0.0 36.1 jit_solution(2620016626573295261)
XLA Ops:
  0.6 33.8 %shard_map.178 = (f32[8,128]{1,0:T(8,128)S(1)}, f32[46,128]{1,0:T(8,128)S(1)}, f32[46,1,128]{2,1,0:T(1,128)S(1)}, f32[46,1,128]{2,1,0:T(1,128)S(1)}, f32[46,128]...) custom-call(f32[1024,384]{1,0:T(8,128)} %refs_0_.1, ...), custom_call_target="tpu_custom_call" | custom-call | tf_op jit(solution)/shard_map/pallas_call | solution.py:565
  34.5 1.4 %shard_map.179 = (f32[1]{0:T(128)}, f32[1]{0:T(128)}, f32[46,128]{1,0:T(8,128)}, f32[46,1,128]{2,1,0:T(1,128)}, f32[46,1,128]{2,1,0:T(1,128)}, /*index=5*/f32[46...) custom-call(f32[8,128]{1,0:T(8,128)S(1)} %get-tuple-element.26.scal, ...), custom_call_target="tpu_custom_call" | custom-call | tf_op jit(solution)/shard_map/pallas_call | solution.py:585

commit v4 on v3

--- a/solution.py
+++ b/solution.py
@@ -107,7 +107,7 @@
 
 WS = {
     "enc_f": (128, 96), "rd_f": (128, 128), "l_f": (128, 192), "ti_f": (128, 512), "to_f": (128, 128), "db_f": (128, 256),
-    "dt_f": (128, 256), "out_f": (96, 128), "out_b": (128, 96), "db_b": (128, 128), "dt_b": (128, 128), "to_b": (128, 128),
+    "dt_f": (128, 256), "out_f": (96, 128), "out_b": (128, 96), "db_b": (64, 256), "dt_b": (128, 128), "to_b": (128, 128),
     "ti_b": (256, 256), "ru_b": (64, 128), "he_b": (128, 256), "book_b": (256, 256), "book_t": (256, 256),
 }
 KEEP = {
@@ -138,7 +138,7 @@
     w["dt_f"][...] = quad(0.5 * t(O_DT, O_RD))
     w["out_f"][...] = stack(f(O_OUT, O_END))
     w["out_b"][...] = pair(0.5 * t(O_OUT, O_END))
-    w["db_b"][...] = stack(f(O_DB, O_DT))
+    w["db_b"][...] = pair(f(O_DB, O_DT))
     w["dt_b"][...] = stack(f(O_DT, O_RD))
     w["to_b"][...] = pair(0.5 * t(O_TO, O_OUT))
     w["ti_b"][...] = pair(f(O_TI, O_DB))
@@ -246,7 +246,7 @@
     gpdb = gpd.astype(bf16)
     gtrb = lanes([sum(gpd[:, R * p : R * p + R] for p in range(4 * g_, 4 * g_ + 4)) for g_ in (0, 1)]).astype(bf16)
     keep["gt"][:, tops] = halves(nn(w["dt_b"][...], gtrb))
-    keep["gl"][i] = halves(nn(w["db_b"][...], gpdb))
+    keep["gl"][i] = nn(w["db_b"][...], twice(gpdb))
     keep["hd"][i] = hdb
     keep["gr"][i] = grb
     keep["gpd"][i] = gpdb
@@ -306,15 +306,17 @@
 def swap_start(axis, n, src_at, buf, sems):
     me = lax.axis_index(axis)
 
-    def go(k, carry):
-        peer = lax.rem(me + k, n)
-        pltpu.make_async_remote_copy(
-            src_ref=src_at(peer), dst_ref=buf.at[me], send_sem=sems[0], recv_sem=sems[1],
-            device_id={axis: peer}, device_id_type=pl.DeviceIdType.MESH,
-        ).start()
+    def go(peer, carry):
+        @pl.when(peer != me)
+        def _():
+            pltpu.make_async_remote_copy(
+                src_ref=src_at(peer), dst_ref=buf.at[me], send_sem=sems[0], recv_sem=sems[1],
+                device_id={axis: peer}, device_id_type=pl.DeviceIdType.MESH,
+            ).start()
+
         return carry
 
-    lax.fori_loop(1, n, go, 0)
+    lax.fori_loop(0, n, go, 0)
 
 
 def swap_wait(axis, n, buf, sems, recv):
@@ -330,6 +332,8 @@
 
 
 def total(v):
+    while v.shape[0] % 16 == 0:
+        v = halves(v)
     return jnp.sum(jnp.sum(v, axis=0, keepdims=True), axis=1, keepdims=True)
 
 
@@ -462,12 +466,11 @@
     each(n, lambda i: add(acc["db"], nt(keep["qb"][i], keep["gpd"][i])))
     put_rows(grad_own, O_DB, halves(acc["db"][...]) * scale)
     put_rows(grad_own, O_DT, halves(nt(keep["qt"][...], keep["gtr"][...])) * scale)
-    share_start((8, 9), grad_own, grad_all, sem_grad)
     each(n, lambda i: add(acc["he"], nt(keep["both"][i], keep["he"][i])))
     put_rows(grad_own, O_RD, acc["he"][64:128] * scale)
     put_rows(grad_own, O_L, (acc["he"][0:64] + exact(cross, p_ref[O_RU:O_TI], ((1,), (0,)))) * scale)
     put_rows(grad_own, O_TO, nt(keep["ht"][...], keep["glt"][...]).T * scale)
-    share_start((12, 13, 10, 11), grad_own, grad_all, sem_grad)
+    share_start((8, 9, 12, 13, 10, 11), grad_own, grad_all, sem_grad)
     each(n, lambda i: add(acc["out"], nt(keep["hd"][i], keep["gr"][i])))
     put_rows(grad_own, O_OUT, acc["out"][...].T * scale)
     share_start((14, 15), grad_own, grad_all, sem_grad)

time: 36.2 us -> 35.1 us (0.970)
  the two profiles are of different devices: /device:TPU:0 before, /device:TPU:1 now
where the time goes in v4:
time: 35.1 us; the launch traced here: 34.5 us
  Pallas kernels  33.7 us (96%)
  between operations  0.81 us (2%)
    pallas_call x1, Pallas kernels, shards(): pl.pallas_call(functools.partial(kernel, R=R), out_shape=tuple((pltpu.VME...  32.2 us
    pallas_call x1, Pallas kernels, shards(): pl.pallas_call(hand_over, out_shape=(shape(1), shape(1)) + tuple((shape(*...  1.41 us

profile of v4, /device:TPU:1, one launch (start us, length us, event | category | flops | bytes accessed | tf_op | source)
XLA Modules:
  0.0 34.5 jit_solution(12627967031846991948)
XLA Ops:
  0.6 32.2 %shard_map.178 = (f32[8,128]{1,0:T(8,128)S(1)}, f32[46,128]{1,0:T(8,128)S(1)}, f32[46,1,128]{2,1,0:T(1,128)S(1)}, f32[46,1,128]{2,1,0:T(1,128)S(1)}, f32[46,128]...) custom-call(f32[1024,384]{1,0:T(8,128)} %refs_0_.1, ...), custom_call_target="tpu_custom_call" | custom-call | tf_op jit(solution)/shard_map/pallas_call | solution.py:568
  32.9 1.4 %shard_map.179 = (f32[1]{0:T(128)}, f32[1]{0:T(128)}, f32[46,128]{1,0:T(8,128)}, f32[46,1,128]{2,1,0:T(1,128)}, f32[46,1,128]{2,1,0:T(1,128)}, /*index=5*/f32[46...) custom-call(f32[8,128]{1,0:T(8,128)S(1)} %get-tuple-element.26.scal, ...), custom_call_target="tpu_custom_call" | custom-call | tf_op jit(solution)/shard_map/pallas_call | solution.py:588

commit v5 on v4

--- a/solution.py
+++ b/solution.py
@@ -303,7 +303,7 @@
     return w, keep, acc, codes, scratch
 
 
-def swap_start(axis, n, src_at, buf, sems):
+def swap_start(axis, n, src_at, buf, sems, at=0):
     me = lax.axis_index(axis)
 
     def go(peer, carry):
@@ -316,7 +316,7 @@
 
         return carry
 
-    lax.fori_loop(0, n, go, 0)
+    lax.fori_loop(at, n, go, 0)
 
 
 def swap_wait(axis, n, buf, sems, recv):
@@ -346,6 +346,7 @@
 N_DP = 16
 N_REP = 8
 SHARE = 46
+FIRST = 1
 def share_start(shares, src, buf, sems):
     me = lax.axis_index("dp")
     for s in shares:
@@ -482,6 +483,8 @@
         par_share[s, 0:SHARE] = p_ref[SHARE * s : SHARE * s + SHARE]
     swap_wait("dp", N_DP, part_all, sem_part, True)
     sums_all[dp] = in_order(part_all, N_DP)
+    sums_src = lambda peer: sums_all.at[dp]
+    swap_start("dp", FIRST, sums_src, sums_all, sem_sums)
     swap_wait("dp", N_DP, stat_all, sem_stat, True)
     stats = in_order(stat_all, N_DP)
     seen = jnp.concatenate([lanes([stats[4 * level + j : 4 * level + j + 1] for j in range(4)]) for level in (0, 1)], axis=0)
@@ -504,8 +507,7 @@
     step_all[rep, SHARE:48] = jnp.zeros((48 - SHARE, 128), f32)
     step_src = lambda peer: step_all.at[rep]
     swap_start("rep", N_REP, step_src, step_all, sem_step)
-    sums_src = lambda peer: sums_all.at[dp]
-    swap_start("dp", N_DP, sums_src, sums_all, sem_sums)
+    swap_start("dp", N_DP, sums_src, sums_all, sem_sums, FIRST)
 
     first_out[:, 0, :] = first_new
     second_out[:, 0, :] = second_new

time: 35.1 us -> 34.7 us (0.989); the launches traced: 34.5 us -> 34.6 us
  no operation moved by 1% of the time
where the time goes in v5:
time: 34.7 us; the launch traced here: 34.6 us
  Pallas kernels  33.8 us (97%)
  between operations  0.81 us (2%)
    pallas_call x1, Pallas kernels, shards(): pl.pallas_call(functools.partial(kernel, R=R), out_shape=tuple((pltpu.VME...  32.4 us
    pallas_call x1, Pallas kernels, shards(): pl.pallas_call(hand_over, out_shape=(shape(1), shape(1)) + tuple((shape(*...  1.41 us

profile of v5, /device:TPU:1, one launch (start us, length us, event | category | flops | bytes accessed | tf_op | source)
XLA Modules:
  0.0 34.6 jit_solution(7611229820187475449)
XLA Ops:
  0.6 32.4 %shard_map.178 = (f32[8,128]{1,0:T(8,128)S(1)}, f32[46,128]{1,0:T(8,128)S(1)}, f32[46,1,128]{2,1,0:T(1,128)S(1)}, f32[46,1,128]{2,1,0:T(1,128)S(1)}, f32[46,128]...) custom-call(f32[1024,384]{1,0:T(8,128)} %refs_0_.1, ...), custom_call_target="tpu_custom_call" | custom-call | tf_op jit(solution)/shard_map/pallas_call | solution.py:570
  33.0 1.4 %shard_map.179 = (f32[1]{0:T(128)}, f32[1]{0:T(128)}, f32[46,128]{1,0:T(8,128)}, f32[46,1,128]{2,1,0:T(1,128)}, f32[46,1,128]{2,1,0:T(1,128)}, /*index=5*/f32[46...) custom-call(f32[8,128]{1,0:T(8,128)S(1)} %get-tuple-element.26.scal, ...), custom_call_target="tpu_custom_call" | custom-call | tf_op jit(solution)/shard_map/pallas_call | solution.py:590

commit v6 on v5

--- a/solution.py
+++ b/solution.py
@@ -385,15 +385,15 @@
     x_ref, m_ref, cb_ref, ct_ref, p_ref, first_ref, second_ref, mom_ref, cnt_ref, ema_ref, book_ref = inputs
     w, keep, acc, codes, scratch = unscratch(scratch)
     (
-        lacc, valid_own, valid_all, stat_own, stat_all, grad_own, grad_all, part_own, part_all, sums_all, step_all,
+        lacc, valid_own, valid_all, grad_own, grad_all, part_own, part_all, sums_all, step_all,
         par_share, in_sems, *sems,
     ) = scratch
     loads = [pltpu.make_async_copy(a, b, in_sems.at[i]) for i, (a, b) in enumerate(zip(sources, inputs))]
     load_x, load_m, load_cb, load_ct, load_p, *load_rest, load_book = loads
     for load in (load_p, load_x, load_cb, load_ct, load_book, load_m, *load_rest):
         load.start()
-    sems = [(sems[2 * i], sems[2 * i + 1]) for i in range(6)]
-    sem_valid, sem_stat, sem_grad, sem_part, sem_sums, sem_step = sems
+    sems = [(sems[2 * i], sems[2 * i + 1]) for i in range(5)]
+    sem_valid, sem_grad, sem_part, sem_sums, sem_step = sems
     dp = lax.axis_index("dp")
     rep = lax.axis_index("rep")
     rows = x_ref.shape[0]
@@ -421,7 +421,13 @@
     each(n, lambda i: encoder(i, R, x_ref, codes, w, keep, acc))
 
     load_m.wait()
-    valid_own[...] = jnp.broadcast_to(total(m_ref[...].astype(f32)), (8, 128))
+    valid = jnp.broadcast_to(total(m_ref[...].astype(f32)), (8, 128))
+    valid_own[...] = jnp.concatenate(
+        [
+            acc[name][128 + a : 129 + a, 128 * j : 128 * j + 128]
+            for name in ("sum_b", "sum_t") for a in (0, 1) for j in (0, 1)
+        ] + [valid], axis=0
+    )
     valid_all[dp] = valid_own[...]
     valid_src = lambda peer: valid_own
     pl.semaphore_wait(barrier, N_DP + N_REP - 2)
@@ -432,22 +438,14 @@
         part_own[d] = lanes([acc[name][at : at + 8], acc[name][64 + at : 72 + at]])
     part_src = lambda peer: part_own.at[peer]
     swap_start("dp", N_DP, part_src, part_all, sem_part)
-    stat_own[...] = jnp.concatenate(
-        [
-            acc[name][128 + a : 129 + a, 128 * j : 128 * j + 128]
-            for name in ("sum_b", "sum_t") for a in (0, 1) for j in (0, 1)
-        ], axis=0
-    )
-    stat_src = lambda peer: stat_own
-    swap_start("dp", N_DP, stat_src, stat_all, sem_stat)
     part_all[dp] = part_own[dp]
-    stat_all[dp] = stat_own[...]
 
     each(n, lambda i: decoder(i, R, m_ref, codes, w, keep, acc, lacc))
 
     group_rows = rows * 8 * N_DP
     swap_wait("dp", N_DP, valid_all, sem_valid, True)
-    count = in_order(valid_all, N_DP)[0:1, 0:1]
+    stats = in_order(valid_all, N_DP)
+    count = stats[8:9, 0:1]
     scale = 2.0 / count
     kb = beta_commit / (group_rows * EMB) * count
     kt = beta_commit / (group_rows // 4 * EMB) * count
@@ -485,8 +483,6 @@
     sums_all[dp] = in_order(part_all, N_DP)
     sums_src = lambda peer: sums_all.at[dp]
     swap_start("dp", FIRST, sums_src, sums_all, sem_sums)
-    swap_wait("dp", N_DP, stat_all, sem_stat, True)
-    stats = in_order(stat_all, N_DP)
     seen = jnp.concatenate([lanes([stats[4 * level + j : 4 * level + j + 1] for j in range(4)]) for level in (0, 1)], axis=0)
     counts_new = ema_decay * cnt_ref[...] + (1.0 - ema_decay) * seen
     counts_out[0] = counts_new
@@ -535,7 +531,7 @@
 
     for axis, size, buf, sem in (
         ("dp", N_DP, valid_all, sem_valid), ("dp", N_DP, grad_all, sem_grad), ("dp", N_DP, part_all, sem_part),
-        ("dp", N_DP, stat_all, sem_stat), ("rep", N_REP, step_all, sem_step), ("dp", N_DP, sums_all, sem_sums),
+        ("rep", N_REP, step_all, sem_step), ("dp", N_DP, sums_all, sem_sums),
     ):
         swap_wait(axis, size, buf, sem, False)
 
@@ -575,13 +571,12 @@
         scratch_shapes=[pltpu.VMEM(v.shape, v.dtype) for v in args]
         + scratches(rows, R)
         + [
-            pltpu.VMEM((8, 128), f32), pltpu.VMEM((N_DP, 8, 128), f32),
-            pltpu.VMEM((8, 128), f32), pltpu.VMEM((N_DP, 8, 128), f32),
+            pltpu.VMEM((16, 128), f32), pltpu.VMEM((N_DP, 16, 128), f32),
             pltpu.VMEM((N_DP, 48, 128), f32), pltpu.VMEM((N_DP, 48, 128), f32),
             pltpu.VMEM((N_DP, 8, 512), f32), pltpu.VMEM((N_DP, 8, 512), f32), pltpu.VMEM((N_DP, 8, 512), f32),
             pltpu.VMEM((N_REP, 48, 128), f32), pltpu.VMEM((N_DP, 48, 128), f32), dma((11,)),
         ]
-        + [dma] * 12,
+        + [dma] * 10,
         compiler_params=pltpu.CompilerParams(
             vmem_limit_bytes=60 * 2**20, collective_id=0, has_side_effects=True
         ),

time: 34.7 us -> 35 us (level)
  no operation moved by 1% of the time
where the time goes in v6:
time: 35 us; the launch traced here: 34.9 us
  Pallas kernels  34 us (97%)
  between operations  0.81 us (2%)
    pallas_call x1, Pallas kernels, shards(): pl.pallas_call(functools.partial(kernel, R=R), out_shape=tuple((pltpu.VME...  32.6 us
    pallas_call x1, Pallas kernels, shards(): pl.pallas_call(hand_over, out_shape=(shape(1), shape(1)) + tuple((shape(*...  1.41 us

profile of v6, /device:TPU:1, one launch (start us, length us, event | category | flops | bytes accessed | tf_op | source)
XLA Modules:
  0.0 34.9 jit_solution(6494049743323510001)
XLA Ops:
  0.6 32.6 %shard_map.178 = (f32[8,128]{1,0:T(8,128)S(1)}, f32[46,128]{1,0:T(8,128)S(1)}, f32[46,1,128]{2,1,0:T(1,128)S(1)}, f32[46,1,128]{2,1,0:T(1,128)S(1)}, f32[46,128]...) custom-call(f32[1024,384]{1,0:T(8,128)} %refs_0_.1, ...), custom_call_target="tpu_custom_call" | custom-call | tf_op jit(solution)/shard_map/pallas_call | solution.py:566
  33.3 1.4 %shard_map.179 = (f32[1]{0:T(128)}, f32[1]{0:T(128)}, f32[46,128]{1,0:T(8,128)}, f32[46,1,128]{2,1,0:T(1,128)}, f32[46,1,128]{2,1,0:T(1,128)}, /*index=5*/f32[46...) custom-call(f32[8,128]{1,0:T(8,128)S(1)} %get-tuple-element.26.scal, ...), custom_call_target="tpu_custom_call" | custom-call | tf_op jit(solution)/shard_map/pallas_call | solution.py:585
